TPU v7x, 32 devices: a whole 2x2x4 slice. The times are simulated.
32 devices in a mesh: fsdp: 4 (over z), tensor: 8 (over y, x, core).
Axes of the slice: x: 2, y: 2, z: 4, core: 2. Of those that a mesh axis runs over, the one named last changes fastest.
Arguments:
- momentum: float32 [4, 1152, 7168], P(None, 'fsdp', 'tensor'), may hold values from -600 to 600
- gradient: float32 [4, 1152, 7168], P(None, 'fsdp', 'tensor'), may hold values from -600 to 600
- live_ranks: int32 [4], replicated, may hold values from 0 to 1, as said below
- owner_group: int32 [4], replicated, may hold values from 0 to 3, each once
- row_counts: int32 [4, 4], replicated, may hold values from 1 to 288, as said below
- row_offsets: int32 [4, 4], replicated, may hold values from 0 to 575, as said below
Outputs:
- new_momentum: float32 [4, 1152, 7168], P(None, 'fsdp', 'tensor')
- update_shards: float32 [4, 1152, 7168], P(None, 'fsdp', 'tensor')
- owned_update: float32 [4, 576, 7168], P('fsdp', None, 'tensor')
Inputs may be any that keep to these rules, and one draw needn't show every extreme that they name: `live_ranks`: exactly one rank is dead. For every matrix the live ranks' segments [row_offsets, row_offsets + row_counts) are disjoint and cover all 576 rows, and one live rank holds exactly 288 rows. The dead rank's entries are stale and describe no rows. `row_offsets`: see row_counts.
All inputs are finite; a program needn't handle non-finite values.
Results may differ from a plain program's by a relative error of at most 0.0003.
Values sent between devices are 32-bit elements; how exact they have to be, the bound alone decides.
No kernel may reach another device: no remote copies, remote signals or barrier semaphores. Data moves between devices by JAX's collectives and lax.ppermute only.
A program may use at most 64 MiB of HBM per device.

v0:
```python
import functools
import math

import jax
import jax.numpy as jnp
from jax import lax
from jax.experimental import pallas as pl
from jax.experimental.pallas import tpu as pltpu
from jax.sharding import PartitionSpec as P

WIDTH = 7168
INNER = 576
PANEL = INNER // 3
TILE = 256
SUBLANES = 8

MOMENTUM_RATE = 0.95
QUINTIC_FIRST = 3.4445
QUINTIC_SECOND = -4.775
QUINTIC_THIRD = 2.0315
EPSILON = 1e-07
OUT_SCALE = 0.2 * math.sqrt(max(INNER, WIDTH))
SMALL = pltpu.CompilerParams(vmem_limit_bytes=1024 * 1024)
FULL = pltpu.CompilerParams(vmem_limit_bytes=60 * 1024 * 1024)
PARAMS = pltpu.CompilerParams(vmem_limit_bytes=24 * 1024 * 1024)
HBM = pl.BlockSpec(memory_space=pltpu.HBM)
ANY = pl.BlockSpec(memory_space=pl.ANY)
VMEM = pl.BlockSpec(memory_space=pltpu.VMEM)


def halves(value):
    high = value.astype(jnp.bfloat16)
    low = (value - high.astype(jnp.float32)).astype(jnp.bfloat16)
    return high, low


def dot(left, right, contract=((1,), (0,))):
    return lax.dot_general(left, right, (contract, ((), ())), preferred_element_type=jnp.float32)


DEPTH = INNER // TILE * TILE
PARTS = [(side, rows) for rows in ((0, DEPTH), (DEPTH, INNER)) if rows[0] < rows[1] for side in (1, 0, 0)]


def passes_left(value):
    high, low = halves(value)
    return jnp.concatenate(
        [part[:, first:last] for first, last in ((0, DEPTH), (DEPTH, INNER)) for part in (high, low, high)], axis=1
    )


def passes_right(value):
    sides = halves(value)
    return jnp.concatenate([sides[side][first:last] for side, (first, last) in PARTS], axis=0)


def is_inner(rank, ranks):
    low = ranks // 4
    return (rank >= low) & (rank < ranks - low)


def mate(ranks):
    return ranks // 4


def table_scratch(matrices, ranks):
    return [
        pltpu.SMEM((matrices,), jnp.int32),
        pltpu.SMEM((ranks,), jnp.int32),
        pltpu.SMEM((matrices, ranks), jnp.int32),
        pltpu.SMEM((matrices, ranks), jnp.int32),
        pltpu.SemaphoreType.DMA((4,)),
    ]


def table_jobs(tables, held):
    *places, arrive = held
    copies = [
        pltpu.make_async_copy(table, place, arrive.at[index])
        for index, (table, place) in enumerate(zip(tables, places))
    ]
    return copies, places


def fetch_tables(tables, held):
    copies, places = table_jobs(tables, held)
    for copy in copies:
        copy.start()
    for copy in copies:
        copy.wait()
    return places


def matrix_of(owner_group, rank):
    found = jnp.int32(0)
    for matrix in range(owner_group.shape[0]):
        found = jnp.where(owner_group[matrix] == rank, matrix, found)
    return found


def over_tiles(tiles, body, carry):
    group = next(group for group in (6, 3, 2, 1) if tiles % group == 0)

    def step(index, carry):
        for member in range(group):
            carry = body(index * group + member, carry)
        return carry

    return lax.fori_loop(0, tiles // group, step, carry)


def each_copy(copies, action):
    for condition, source, place, flag in copies:

        @pl.when(condition)
        def _(source=source, place=place, flag=flag):
            getattr(pltpu.make_async_copy(source, place, flag), action)()


def blend_kernel(first, chunks, *refs):
    tables, (momentum, gradient) = refs[:4], refs[4:6]
    ranks = tables[1].shape[0]
    *outs, token, olds, grads, arrive, leave = refs[-ranks - 10 + first : -5]
    owner_group, live_ranks, row_counts, _ = fetch_tables(tables, refs[-5:])
    rank = lax.axis_index("fsdp")
    slots, columns = outs[0].shape
    size = slots // chunks
    jobs = []
    for step in range(1, ranks + 1):
        step = step % ranks
        if first and step == 0:
            continue
        target = rank ^ step
        wanted = is_inner(target, ranks)
        matrix = matrix_of(owner_group, target ^ mate(ranks) if first else target)
        if first and step == mate(ranks):
            matrix = matrix_of(owner_group, jnp.where(wanted, rank, target))
            wanted = rank >= 0
        count = row_counts[matrix, rank] * live_ranks[rank]
        for chunk in range(chunks):
            part = pl.ds(chunk * size, size)
            flags = arrive.at[step, chunk, 0], arrive.at[step, chunk, 1]
            incoming = (
                (wanted, momentum.at[matrix, part], olds.at[step, part], flags[0]),
                (wanted, gradient.at[matrix, part], grads.at[step, part], flags[1]),
            )
            outgoing = (wanted, olds.at[step, part], outs[step - first].at[part], leave.at[step, chunk])
            jobs.append((step, chunk, count, incoming, outgoing))
            each_copy(incoming, "start")
    token[...] = jnp.zeros_like(token)
    for step, chunk, count, incoming, outgoing in jobs:

        @pl.when(incoming[0][0])
        def _(step=step, chunk=chunk, count=count, incoming=incoming, outgoing=outgoing):
            for _, source, place, flag in incoming:
                pltpu.make_async_copy(source, place, flag).wait()
            sublane = lax.broadcasted_iota(jnp.int32, (SUBLANES, columns), 0)

            def tile(index, carry):
                first_row = chunk * size + index * SUBLANES
                rows = pl.ds(pl.multiple_of(first_row, SUBLANES), SUBLANES)
                grad_now = grads[step, rows, :]
                fresh = MOMENTUM_RATE * olds[step, rows, :] + grad_now
                olds[step, rows, :] = jnp.where(sublane < count - first_row, grad_now + MOMENTUM_RATE * fresh, 0.0)
                return carry

            over_tiles(size // SUBLANES, tile, 0)
            pltpu.make_async_copy(*outgoing[1:]).start()

    each_copy([job[-1] for job in jobs], "wait")


def fresh_kernel(live_ranks, row_counts, momentum, gradient, _, out, token):
    token[...] = jnp.zeros_like(token)
    rank, matrix = lax.axis_index("fsdp"), pl.program_id(0)
    slots, columns = out.shape
    count = row_counts[matrix, rank] * live_ranks[rank]
    sublane = lax.broadcasted_iota(jnp.int32, (SUBLANES, columns), 0)

    def tile(index, carry):
        rows = pl.ds(pl.multiple_of(index * SUBLANES, SUBLANES), SUBLANES)
        fresh = MOMENTUM_RATE * momentum[rows, :] + gradient[rows, :]
        out[rows, :] = jnp.where(sublane < count - index * SUBLANES, fresh, 0.0)
        return carry

    over_tiles(slots // SUBLANES, tile, 0)


def assemble(blocks, landed, padded, arrive, tables, held, first):
    ranks, slots, columns = landed.shape
    copies = []
    for step in range(ranks):
        copies.append(pltpu.make_async_copy(blocks[step], landed.at[step], arrive.at[step]))
        copies[-1].start()
    owner_group, _, _, row_offsets = fetch_tables(tables, held)
    rank = lax.axis_index("fsdp")
    base = jnp.where(is_inner(rank, ranks), rank, rank ^ mate(ranks))
    matrix = matrix_of(owner_group, base ^ mate(ranks) if first else base)
    padded[...] = jnp.zeros_like(padded)
    sublane = lax.broadcasted_iota(jnp.int32, (SUBLANES, columns), 0)
    for step in range(ranks):
        start = row_offsets[matrix, base ^ step]
        shift = start % SUBLANES
        origin = start - shift
        copies[step].wait()

        def tile(index, before, origin=origin, shift=shift, step=step):
            moved = pltpu.roll(landed[step, pl.ds(pl.multiple_of(index * SUBLANES, SUBLANES), SUBLANES), :], shift, 0)
            rows = pl.ds(pl.multiple_of(origin + index * SUBLANES, SUBLANES), SUBLANES)
            padded[rows, :] = padded[rows, :] + jnp.where(sublane < shift, before, moved)
            return moved

        after = over_tiles(slots // SUBLANES, tile, jnp.zeros((SUBLANES, columns), jnp.float32))
        rows = pl.ds(pl.multiple_of(origin + slots, SUBLANES), SUBLANES)
        padded[rows, :] = padded[rows, :] + jnp.where(sublane < shift, after, 0.0)


def gram_kernel(inner, first, ranks, *refs):
    pair, keep, send = refs[-15:-12]
    landed, padded, high_held, low_held, gram, arrive, leave = refs[-12:-5]

    @pl.when(is_inner(lax.axis_index("fsdp"), ranks) == inner)
    def _():
        assemble(refs[4 : 4 + ranks], landed, padded, arrive, refs[:4], refs[-5:], first)
        high, low = halves(padded[:INNER, :])
        high_held[...] = high
        low_held[...] = low
        outgoing = [
            pltpu.make_async_copy(high_held, pair.at[0], leave.at[0]),
            pltpu.make_async_copy(low_held, pair.at[1], leave.at[1]),
        ]
        for copy in outgoing:
            copy.start()
        left = jnp.concatenate([high, low, high], axis=1)
        right = jnp.concatenate([low, high, high], axis=1)
        for panel in range(3):
            here = slice(panel * PANEL, (panel + 1) * PANEL)
            store_panel(gram, panel, dot(left[panel * PANEL :], right[here], ((1,), (1,))))
        mine, other = core_rows()
        keep[...] = gram[mine, :]
        send[...] = gram[other, :]
        for copy in outgoing:
            copy.wait()


def core_rows():
    half = INNER // 2
    first = (lax.axis_index("tensor") & 1) * half
    return tuple(pl.ds(pl.multiple_of(start, SUBLANES), half) for start in (first, half - first))


def store_panel(packed, panel, part):
    if panel == 0:
        packed[:, :PANEL] = part
    elif panel == 1:
        packed[: 2 * PANEL, PANEL:] = part
    else:
        packed[2 * PANEL :, PANEL:] = part


def unpack(packed, gram):
    gram[:, :PANEL] = packed[:, :PANEL]
    gram[PANEL:, PANEL : 2 * PANEL] = packed[: 2 * PANEL, PANEL:]
    gram[2 * PANEL :, 2 * PANEL :] = packed[2 * PANEL :, PANEL:]
    gram[:PANEL, PANEL:] = packed[PANEL:, :PANEL].T
    gram[PANEL : 2 * PANEL, 2 * PANEL :] = packed[PANEL : 2 * PANEL, PANEL:].T
    return gram[...]


def symmetric_product(left, right, out):
    for begin in range(0, INNER, TILE):
        end = min(begin + TILE, INNER)
        part = dot(left[begin:], right[:, begin:end])
        out[begin:, begin:end] = part
        if end < INNER:
            out[begin:end, end:] = part[end - begin :].T
    return out[...]


def polynomial(raw, gram):
    diagonal = lax.broadcasted_iota(jnp.int32, raw.shape, 0) == lax.broadcasted_iota(jnp.int32, raw.shape, 1)
    square_total = jnp.sum(jnp.where(diagonal, raw, 0.0))
    norm = jnp.sqrt(jnp.full((1, 1), square_total, jnp.float32)) + EPSILON
    inverse = 1.0 / norm
    first = (raw * inverse) * inverse
    first_right = passes_right(first)
    second = symmetric_product(passes_left(first), first_right, gram)
    base = QUINTIC_SECOND * first + QUINTIC_THIRD * second + jnp.where(diagonal, QUINTIC_FIRST, 0.0)
    base_left = passes_left(base)
    third = symmetric_product(base_left, first_right, gram)
    next_gram = symmetric_product(base_left, passes_right(third), gram)
    square = symmetric_product(passes_left(next_gram), passes_right(next_gram), gram)
    outer = QUINTIC_SECOND * next_gram + QUINTIC_THIRD * square + jnp.where(diagonal, QUINTIC_FIRST, 0.0)
    return symmetric_product(passes_left(outer), passes_right(base), gram) * (inverse * OUT_SCALE)


def extract(padded, start, count, staged, step):
    _, slots, columns = staged.shape
    sublane = lax.broadcasted_iota(jnp.int32, (SUBLANES, columns), 0)
    shift = start % SUBLANES
    base = start - shift
    back = jnp.where(shift == 0, 0, SUBLANES - shift)

    def window(index):
        rows = pl.ds(pl.multiple_of(base + index * SUBLANES, SUBLANES), SUBLANES)
        return pltpu.roll(padded[rows, :], back, 0)

    def tile(index, here):
        after = window(index + 1)
        moved = jnp.where(sublane < SUBLANES - shift, here, after)
        rows = pl.ds(pl.multiple_of(index * SUBLANES, SUBLANES), SUBLANES)
        staged[step, rows, :] = jnp.where(sublane < count - index * SUBLANES, moved, 0.0)
        return after

    over_tiles(slots // SUBLANES, tile, window(0))


def stack_jobs(pair, stacked, arrive):
    jobs, begin = [], 0
    for index, (side, (first_row, last_row)) in enumerate(PARTS):
        size = last_row - first_row
        source = pair.at[side, pl.ds(first_row, size)]
        jobs.append((source, stacked.at[pl.ds(begin, size)], arrive.at[index]))
        begin += size
    return jobs


def update_kernel(first, steps, *refs):
    tables, (keep, away, pair) = refs[:4], refs[4:7]
    gram, padded, staged, stacked, held, arrive, leave = refs[-12:-5]
    whole, *homes = refs[-13 - len(steps) : -12]
    ranks = tables[1].shape[0]
    rank = lax.axis_index("fsdp")
    incoming = [pltpu.make_async_copy(*job) for job in stack_jobs(pair, stacked, arrive)] if steps else []
    for copy in incoming:
        copy.start()
    table_copies, places = table_jobs(tables, refs[-5:])
    for copy in table_copies:
        copy.start()
    mine, other = core_rows()
    held[mine, :] = keep[...]
    held[other, :] = away[...]
    total = polynomial(unpack(held, gram), gram)
    for panel in range(3):
        store_panel(held, panel, total[panel * PANEL :, panel * PANEL : (panel + 1) * PANEL])
    copies = [pltpu.make_async_copy(held, whole, leave.at[len(steps)])]
    copies[0].start()
    for copy in [*incoming, *table_copies]:
        copy.wait()
    if steps:
        padded[:INNER, :] = dot(passes_left(total), stacked[...])
    owner_group, live_ranks, row_counts, row_offsets = places
    matrix = matrix_of(owner_group, rank ^ mate(ranks) if first else rank)
    for index, step in enumerate(steps):
        target = rank ^ step
        count = row_counts[matrix, target] * live_ranks[target]
        extract(padded, row_offsets[matrix, target], count, staged, index)
        copies.append(pltpu.make_async_copy(staged.at[index], homes[index], leave.at[index]))
        copies[-1].start()
    for copy in copies:
        copy.wait()


def finish_kernel(ranks, *refs):
    tables, sources = refs[:4], refs[4:10]
    (result, shards, gram, padded, staged, stacked, held, arrive, leave), refs = refs[11:20], refs[20:]
    rank = lax.axis_index("fsdp")
    owner_group, live_ranks, row_counts, row_offsets = fetch_tables(tables, refs)

    inner = is_inner(rank, ranks)
    outer = jnp.logical_not(inner)

    def make(index, carry):
        wanted = [jnp.logical_and(inner, index == 1), jnp.logical_and(inner, index == 0), outer]
        incoming = []
        for condition, packed, pair in zip(wanted, sources[::2], sources[1::2]):
            incoming.append((condition, packed, held, leave.at[2]))
            incoming += [(condition, *job) for job in stack_jobs(pair, stacked, arrive)]
        each_copy(incoming, "start")
        each_copy(incoming, "wait")
        padded[:INNER, :] = dot(passes_left(unpack(held, gram)), stacked[...])
        matrix = matrix_of(owner_group, rank ^ (index * mate(ranks)))
        extract(padded, row_offsets[matrix, rank], row_counts[matrix, rank] * live_ranks[rank], staged, 0)
        outgoing = [
            (index >= 0, staged.at[0], shards.at[matrix], leave.at[0]),
            (index == 0, padded.at[pl.ds(0, INNER)], result, leave.at[1]),
        ]
        each_copy(outgoing, "start")
        each_copy(outgoing, "wait")
        return carry

    lax.fori_loop(0, jnp.where(inner, 2, 1), make, 0)


def place_kernel(first, ranks, steps, *refs):
    table, blocks, shards = refs[0], refs[1 : 1 + len(steps)], refs[2 + len(steps)]
    owner_group, arrive, leave = refs[3 + len(steps) :]
    rank = lax.axis_index("fsdp")
    fetch = pltpu.make_async_copy(table, owner_group, arrive)
    fetch.start()
    fetch.wait()
    copies = []
    for index, step in enumerate(steps):
        source = rank ^ step
        matrix = matrix_of(owner_group, source ^ mate(ranks) if first else source)
        copies.append((is_inner(source, ranks), blocks[index], shards.at[matrix], leave.at[index]))
    each_copy(copies, "start")
    each_copy(copies, "wait")


def idle_kernel(*refs):
    pass


def floats(*shape):
    return jax.ShapeDtypeStruct(shape, jnp.float32)


def vmem(*shape, dtype=jnp.float32):
    return pltpu.VMEM(shape, dtype)


def flags(*shape):
    return pltpu.SemaphoreType.DMA(shape)


FREE = pl.CostEstimate(flops=0, bytes_accessed=0, transcendentals=0)


def blend(first, tables, momentum, gradient, before):
    _, slots, columns = momentum.shape
    ranks = tables[1].shape[0]
    chunks = 2 if slots % (2 * SUBLANES) == 0 else 1
    return pl.pallas_call(
        functools.partial(blend_kernel, first, chunks),
        out_shape=[floats(slots, columns)] * (ranks - first) + [floats(SUBLANES, 128)],
        in_specs=[HBM] * 6 + [ANY] * len(before),
        out_specs=[ANY] * (ranks - first) + [VMEM],
        scratch_shapes=[vmem(ranks, slots, columns)] * 2
        + [flags(ranks, chunks, 2), flags(ranks, chunks)]
        + table_scratch(*tables[2].shape),
        compiler_params=FULL,
        cost_estimate=FREE,
        name="blend",
    )(*tables, momentum, gradient, *before)


def fresh_momentum(tables, momentum, gradient, before):
    matrices, slots, columns = momentum.shape
    block = pl.BlockSpec((None, slots, columns), lambda matrix: (matrix, 0, 0))
    return pl.pallas_call(
        fresh_kernel,
        grid=(matrices,),
        out_shape=[floats(*momentum.shape), floats(SUBLANES, 128)],
        in_specs=[pl.BlockSpec(memory_space=pltpu.SMEM)] * 2 + [block] * 2 + [ANY],
        out_specs=[block, pl.BlockSpec((SUBLANES, 128), lambda matrix: (0, 0))],
        compiler_params=FULL,
        cost_estimate=FREE,
        name="fresh_momentum",
    )(*tables[1:3], momentum, gradient, before)


def assemble_and_gram(inner, first, tables, blocks, *after):
    slots, columns = blocks[0].shape
    ranks = len(blocks)
    pair = jax.ShapeDtypeStruct((4, INNER, columns), jnp.bfloat16)
    return pl.pallas_call(
        functools.partial(gram_kernel, inner, first, ranks),
        out_shape=[pair] + [floats(INNER // 2, 2 * PANEL)] * 2,
        in_specs=[HBM] * 4 + [ANY] * (ranks + len(after)),
        out_specs=[ANY, VMEM, VMEM],
        scratch_shapes=[
            vmem(ranks, slots, columns),
            vmem(INNER + slots + SUBLANES, columns),
            vmem(INNER, columns, dtype=jnp.bfloat16),
            vmem(INNER, columns, dtype=jnp.bfloat16),
            vmem(INNER, 2 * PANEL),
            flags(ranks),
            flags(2),
        ]
        + table_scratch(*tables[2].shape),
        compiler_params=PARAMS,
        cost_estimate=FREE,
        name="assemble_and_gram",
    )(*tables, *blocks, *after)


def update_shapes(steps, slots, columns):
    return [floats(INNER, 2 * PANEL)] + [floats(slots, columns)] * len(steps)


def nothing(shapes):
    return pl.pallas_call(
        idle_kernel, out_shape=shapes, out_specs=[ANY] * len(shapes), compiler_params=SMALL, name="nothing"
    )()


def apply_update(first, steps, tables, keep, away, pair, slots, *after):
    columns = pair.shape[2]
    return pl.pallas_call(
        functools.partial(update_kernel, first, steps),
        out_shape=update_shapes(steps, slots, columns),
        in_specs=[HBM] * 4 + [VMEM] * 2 + [ANY] * (1 + len(after)),
        out_specs=[ANY] * (1 + len(steps)),
        scratch_shapes=[
            vmem(INNER, INNER),
            vmem(INNER + slots + 2 * SUBLANES, columns),
            vmem(max(len(steps), 1), slots, columns),
            vmem(3 * INNER, columns, dtype=jnp.bfloat16),
            vmem(INNER, 2 * PANEL),
            flags(len(PARTS)),
            flags(len(steps) + 1),
        ]
        + table_scratch(*tables[2].shape),
        compiler_params=PARAMS,
        cost_estimate=FREE,
        name="apply_update",
    )(*tables, keep, away, pair, *after)


def touch(value, flops=0):
    return pl.pallas_call(
        idle_kernel,
        out_shape=floats(SUBLANES, 128),
        in_specs=[ANY],
        out_specs=ANY,
        compiler_params=SMALL,
        cost_estimate=pl.CostEstimate(flops=flops, bytes_accessed=0, transcendentals=0),
        name="touch",
    )(value)


def finish(tables, sources, shape, after):
    _, slots, columns = shape
    return pl.pallas_call(
        functools.partial(finish_kernel, tables[1].shape[0]),
        out_shape=[floats(INNER, columns), floats(*shape)],
        in_specs=[HBM] * 4 + [ANY] * 7,
        out_specs=[HBM] * 2,
        scratch_shapes=[
            vmem(INNER, INNER),
            vmem(INNER + slots + 2 * SUBLANES, columns),
            vmem(2, slots, columns),
            vmem(3 * INNER, columns, dtype=jnp.bfloat16),
            vmem(INNER, 2 * PANEL),
            flags(len(PARTS)),
            flags(3),
        ]
        + table_scratch(*tables[2].shape),
        compiler_params=PARAMS,
        cost_estimate=FREE,
        name="finish",
    )(*tables, *sources, after)


def place_blocks(first, owner_group, steps, blocks, shards, ranks):
    return pl.pallas_call(
        functools.partial(place_kernel, first, ranks, steps),
        out_shape=floats(*shards.shape),
        in_specs=[HBM] + [VMEM] * len(blocks) + [HBM],
        out_specs=HBM,
        scratch_shapes=[pltpu.SMEM(owner_group.shape, jnp.int32), flags(), flags(len(steps))],
        input_output_aliases={1 + len(blocks): 0},
        compiler_params=PARAMS,
        cost_estimate=FREE,
        name="place_blocks",
    )(owner_group, *blocks, shards)


def sum_halves(keep, send, axis, streams):
    size = lax.axis_size(axis)

    def exchange(piece, bits):
        return lax.ppermute(piece, axis, [(i, i ^ bits[i & 1]) for i in range(size)])

    chips = [1 << shift for shift in range(1, size.bit_length() - 1)]
    keep = keep + exchange(send, (1, 1))
    pieces = jnp.split(keep, streams, axis=0)
    for bits in zip(chips, reversed(chips)):
        pieces = [piece + exchange(piece, bits[:: 1 - 2 * index]) for index, piece in enumerate(pieces)]
    keep = jnp.concatenate(pieces, axis=0)
    return keep, exchange(keep, (1, 1))


def on_device(momentum, gradient, live_ranks, owner_group, row_counts, row_offsets):
    ranks = lax.axis_size("fsdp")
    _, slots, columns = momentum.shape
    inner = is_inner(lax.axis_index("fsdp"), ranks)
    tables = (owner_group, live_ranks, row_counts, row_offsets)
    last = [2, 1, *range(3, ranks)]
    early = [step for step in last if step != mate(ranks)]

    def pairs(step, inward):
        return [(i, i ^ step) for i in range(ranks) if is_inner(i ^ step if inward else i, ranks)]

    def to_inner(block, step):
        return lax.ppermute(block, "fsdp", pairs(step, True))

    def from_inner(block, step):
        return lax.ppermute(block, "fsdp", pairs(step, False))

    near = mate(ranks)
    far = [step for step in last if step != near]
    *blends, token = blend(True, tables, momentum, gradient, [])
    own = blends[near - 1]
    swapped = lax.ppermute(own, "fsdp", [(i, i ^ near) for i in range(ranks)])
    arrived = {step: to_inner(blends[step - 1], step) for step in far}
    *blends, token = blend(False, tables, momentum, gradient, [token, touch(swapped)])
    last_blocks = [blends[0]] + [to_inner(blends[step], step) for step in range(1, ranks)]
    new_momentum, token = fresh_momentum(tables, momentum, gradient, token)
    handed = {step: from_inner(arrived[step], near) for step in far}

    def ordered(base, opposite, others):
        return [{0: base, near: opposite, **others}[step] for step in range(ranks)]

    first_blocks = ordered(own, swapped, arrived)
    pair, keep, send = assemble_and_gram(True, True, tables, first_blocks, *[handed[step] for step in far[1:]])

    def first_update(pair, keep, send, after):
        return apply_update(True, early, tables, *sum_halves(keep, send, "tensor", 1), pair, slots, after)

    def first_skip(*_):
        return nothing(update_shapes(early, slots, columns))

    packed, *homes = lax.cond(inner, first_update, first_skip, pair, keep, send, touch(keep, 10**11))
    first_home = [from_inner(block, step) for step, block in zip(early, homes)]
    pair_shape = jax.ShapeDtypeStruct(pair.shape, pair.dtype)

    def outer_update(*blocks):
        pair, keep, send = assemble_and_gram(False, True, tables, blocks)
        return (pair, *apply_update(True, [], tables, *sum_halves(keep, send, "tensor", 1), pair, slots, keep))

    def outer_skip(*_):
        return tuple(nothing([pair_shape, *update_shapes([], slots, columns)]))

    outer_pair, outer_packed = lax.cond(inner, outer_skip, outer_update, *ordered(swapped, own, handed))

    def last_update(after, *blocks):
        pair, keep, send = assemble_and_gram(True, False, tables, blocks, after)
        return (pair, *apply_update(False, last, tables, *sum_halves(keep, send, "tensor", 2), pair, slots))

    def last_skip(*_):
        return tuple(nothing([pair_shape, *update_shapes(last, slots, columns)]))

    last_pair, last_packed, *homes = lax.cond(inner, last_update, last_skip, outer_packed, *last_blocks)
    last_home = [from_inner(block, step) for step, block in zip(last, homes)]

    sources = [packed, pair, last_packed, last_pair, outer_packed, outer_pair]
    result, shards = finish(tables, sources, momentum.shape, token)
    shards = place_blocks(True, owner_group, early, first_home, shards, ranks)
    for step, block in zip(last, last_home):
        shards = place_blocks(False, owner_group, [step], [block], shards, ranks)
    return (new_momentum, shards, result[None])


def solution(mesh):
    placed = (P(None, "fsdp", "tensor"), P(None, "fsdp", "tensor"), P(), P(), P(), P())
    return jax.shard_map(
        on_device,
        mesh=mesh,
        in_specs=placed,
        out_specs=(P(None, "fsdp", "tensor"), P(None, "fsdp", "tensor"), P("fsdp", None, "tensor")),
        check_vma=False,
    )
```

profile of v0, /device:TPU:0, one launch (start us, length us, event | category | flops | bytes accessed | tf_op | source)
XLA Modules:
  0.0 193.6 jit_solution(14624779506178797581)
XLA Ops:
  0.7 4.8 %blend.2 = (f32[288,896]{1,0:T(8,128)}, f32[288,896]{1,0:T(8,128)}, f32[288,896]{1,0:T(8,128)}, f32[8,128]{1,0:T(8,128)}) custom-call(s32[4]{0:T(128)} %refs_0_.15, s32[4]{0:T(128)} %refs_1_.7, s32[4,4]{1,0:T(4,128)} %refs_2_.7, s32[4,4]{1,0:T(4,128)} %refs_3_.7, f32[4,288,896]{2,1,0:T(8,128)} %momentum.1, f32[4,288,896]{2,1,0:T(8,128)} %gradient.1), custom_call_target="tpu_custom_call" | custom-call | tf_op jit(solution)/shard_map/blend/pallas_call | solution.py:434
  6.2 5.8 %collective-permute-start.14 = (f32[288,896]{1,0:T(8,128)}, f32[288,896]{1,0:T(8,128)S(1)}, u32[]{:S(2)}, u32[]{:S(2)}) collective-permute-start(f32[288,896]{1,0:T(8,128)} %get-tuple-element.115.refs_4_), channel_id=1, source_target_pairs={{0,8},{8,0},{16,24},{24,16},{1,9},{9,1},{17,25},{25,17},{2,10},{10... | collective-permute-start | bytes 3096584 | tf_op jit(solution)/shard_map/ppermute | solution.py:606
  12.1 1.9 collective-permute-start.18
  15.2 20.4 %collective-permute-done.14.refs_0_.refs_5_ = f32[288,896]{1,0:T(8,128)S(1)} collective-permute-done((f32[288,896]{1,0:T(8,128)}, f32[288,896]{1,0:T(8,128)S(1)}, u32[]{:S(2)}, u32[]{:S(2)}) %collective-permute-start.14) | collective-permute-done | bytes 1032224 | tf_op jit(solution)/shard_map/ppermute | solution.py:606
  36.2 4.5 %blend.3 = (f32[288,896]{1,0:T(8,128)}, f32[288,896]{1,0:T(8,128)}, f32[288,896]{1,0:T(8,128)}, f32[288,896]{1,0:T(8,128)}, f32[8,128]{1,0:T(8,128)}) custom-call(s32[4]{0:T(128)S(1)} %copy-done.7, s32[4]{0:T(128)S(1)} %copy-done.9, s32[4,4]{1,0:T(4,128)S(1)} %copy-done.5, s32[4,4]{1,0:T(4,128)S(1)} %copy-done.6, f32[4,288,896]{2,1,0:T(8,128)} %momentum.1, ...), custom_call_target="tpu_custom_call" | custom-call | tf_op jit(solution)/shard_map/blend/pallas_call | solution.py:434
  40.8 5.3 %collective-permute-start.15 = (f32[288,896]{1,0:T(8,128)}, f32[288,896]{1,0:T(8,128)}, u32[]{:S(2)}, u32[]{:S(2)}) collective-permute-start(f32[288,896]{1,0:T(8,128)} %get-tuple-element.119), channel_id=1, source_target_pairs={{0,8},{24,16},{1,9},{25,17},{2,10},{26,18},{3,11},{27,19},{4,12},{... | collective-permute-start | bytes 3096584 | tf_op jit(solution)/shard_map/ppermute | solution.py:597
  46.0 2.3 %collective-permute-start.16 = (f32[288,896]{1,0:T(8,128)}, f32[288,896]{1,0:T(8,128)}, u32[]{:S(2)}, u32[]{:S(2)}) collective-permute-start(f32[288,896]{1,0:T(8,128)} %get-tuple-element.120), channel_id=1, source_target_pairs={{0,16},{24,8},{1,17},{25,9},{2,18},{26,10},{3,19},{27,11},{4,20},{... | collective-permute-start | bytes 3096584 | tf_op jit(solution)/shard_map/ppermute | solution.py:597
  48.3 1.6 collective-permute-start.17
  49.9 7.9 %collective-permute-done.18.refs_6_ = f32[288,896]{1,0:T(8,128)S(1)} collective-permute-done((f32[288,896]{1,0:T(8,128)}, f32[288,896]{1,0:T(8,128)S(1)}, u32[]{:S(2)}, u32[]{:S(2)}) %collective-permute-start.18) | collective-permute-done | bytes 1032224 | tf_op jit(solution)/shard_map/ppermute | solution.py:597
  62.3 19.4 %collective-permute-done.19 = f32[288,896]{1,0:T(8,128)} collective-permute-done((f32[288,896]{1,0:T(8,128)S(1)}, f32[288,896]{1,0:T(8,128)}, u32[]{:S(2)}, u32[]{:S(2)}) %collective-permute-start.19) | collective-permute-done | bytes 1032224 | tf_op jit(solution)/shard_map/ppermute | solution.py:600
  81.7 34.1 %conditional.3 = ((bf16[4,576,896]{2,1,0:T(8,128)(2,1)}, f32[576,384]{1,0:T(8,128)})) conditional(s32[]{:T(128)} %convert_element_type.2, (s32[4]{0:T(128)S(1)}, s32[4]{0:T(128)S(1)}, s32[4,4]{1,0:T(4,128)S(1)}, s32[4,4]{1,0:T(4,128)S(1)}, f32[288,896]{1,0:T(8,128)S(1)}, /*index=5*/f32[288,896]{1,0:T(8,128)}, f32[288,896]{1,0:T(8,128)}, ...), branch_computations={%region_0.0_spmd, %region_1.0_spmd} | conditional | flops 331776 | bytes 27574484 | solution.py:636
  81.7 5.9 %assemble_and_gram.3 = (bf16[4,576,896]{2,1,0:T(8,128)(2,1)S(1)}, f32[288,384]{1,0:T(8,128)S(1)}, f32[288,384]{1,0:T(8,128)S(1)}) custom-call(s32[4]{0:T(128)S(1)} %get-tuple-element.50.refs_0_, s32[4]{0:T(128)S(1)} %get-tuple-element.51.refs_1_, s32[4,4]{1,0:T(4,128)S(1)} %get-tuple-element.52.refs_2_, s32[4,4]{1,0:T(4,128)S(1)} %get-tuple-element.53.refs_3_, ...), custom_call_target="tpu_custom_call" | custom-call | tf_op jit(solution)/shard_map/cond/branch_0_fun/assemble_and_gram/pallas_call | solution.py:467
  87.7 1.8 collective-permute-done
  91.1 6.8 %collective-permute-done.1 = f32[288,384]{1,0:T(8,128)S(1)} collective-permute-done((f32[288,384]{1,0:T(8,128)S(1)}, f32[288,384]{1,0:T(8,128)S(1)}, u32[]{:S(2)}, u32[]{:S(2)}) %collective-permute-start.1) | collective-permute-done | bytes 442400 | tf_op jit(solution)/shard_map/cond/branch_0_fun/ppermute | solution.py:574
  97.9 1.6 collective-permute-start.2
  99.5 6.8 %collective-permute-done.2 = f32[288,384]{1,0:T(8,128)S(1)} collective-permute-done((f32[288,384]{1,0:T(8,128)S(1)}, f32[288,384]{1,0:T(8,128)S(1)}, u32[]{:S(2)}, u32[]{:S(2)}) %collective-permute-start.2) | collective-permute-done | bytes 442400 | tf_op jit(solution)/shard_map/cond/branch_0_fun/ppermute | solution.py:574
  106.4 1.8 collective-permute-done.3.refs_5_
  108.2 7.3 %apply_update.3 = f32[576,384]{1,0:T(8,128)} custom-call(s32[4]{0:T(128)S(1)} %get-tuple-element.50.refs_0_, s32[4]{0:T(128)S(1)} %get-tuple-element.51.refs_1_, s32[4,4]{1,0:T(4,128)S(1)} %get-tuple-element.52.refs_2_, s32[4,4]{1,0:T(4,128)S(1)} %get-tuple-element.53.refs_3_, f32[288,384]{1,0:T(8,128)S(1)} %add.24.refs_4_, ...), custom_call_target="tpu_custom_call" | custom-call | tf_op jit(solution)/shard_map/cond/branch_0_fun/apply_update/pallas_call | solution.py:500
  115.7 1.6 collective-permute-start.26
  120.8 5.9 %fresh_momentum.1 = (f32[4,288,896]{2,1,0:T(8,128)}, f32[8,128]{1,0:T(8,128)}) custom-call(s32[4]{0:T(128)} %refs_1_.7, s32[4,4]{1,0:T(4,128)} %refs_2_.7, f32[4,288,896]{2,1,0:T(8,128)} %momentum.1, f32[4,288,896]{2,1,0:T(8,128)} %gradient.1, f32[8,128]{1,0:T(8,128)} %get-tuple-element.116._), custom_call_target="tpu_custom_call" | custom-call | tf_op jit(solution)/shard_map/fresh_momentum/pallas_call | solution.py:451
  127.4 7.4 %finish.1 = (f32[576,896]{1,0:T(8,128)}, f32[4,288,896]{2,1,0:T(8,128)}) custom-call(s32[4]{0:T(128)} %refs_0_.15, s32[4]{0:T(128)} %refs_1_.7, s32[4,4]{1,0:T(4,128)} %refs_2_.7, s32[4,4]{1,0:T(4,128)} %refs_3_.7, f32[576,384]{1,0:T(8,128)} %get-tuple-element.133.refs_4_, bf16[4,576,896]{2,1,0:T(8,128)(2,1)} %get-tuple-element.130.refs_5_, ...), custom_call_target="tpu_custom_call" | custom-call | tf_op jit(solution)/shard_map/finish/pallas_call | solution.py:535
  134.8 2.8 %place_blocks.4.refs_2_ = f32[4,288,896]{2,1,0:T(8,128)} custom-call(s32[4]{0:T(128)S(1)} %copy-done.8, f32[288,896]{1,0:T(8,128)S(1)} %collective-permute-done.25.refs_1_, f32[288,896]{1,0:T(8,128)} %collective-permute-done.26.refs_2_, f32[4,288,896]{2,1,0:T(8,128)} %get-tuple-element.138.refs_3_), custom_call_target="tpu_custom_call", output_to_operand_aliasing={{}: (3, {})} | custom-call | tf_op jit(solution)/shard_map/place_blocks/pallas_call | solution.py:557
  137.6 32.7 %collective-permute-done.24.refs_1_ = f32[288,896]{1,0:T(8,128)S(1)} collective-permute-done((f32[288,896]{1,0:T(8,128)}, f32[288,896]{1,0:T(8,128)S(1)}, u32[]{:S(2)}, u32[]{:S(2)}) %collective-permute-start.24) | collective-permute-done | bytes 1032224 | tf_op jit(solution)/shard_map/ppermute | solution.py:600
  171.8 19.6 %collective-permute-done.23.refs_1_ = f32[288,896]{1,0:T(8,128)S(1)} collective-permute-done((f32[288,896]{1,0:T(8,128)}, f32[288,896]{1,0:T(8,128)S(1)}, u32[]{:S(2)}, u32[]{:S(2)}) %collective-permute-start.23) | collective-permute-done | bytes 1032224 | tf_op jit(solution)/shard_map/ppermute | solution.py:600
  (51 shorter events, 16.6 us)
Async XLA Ops:
  0.6 35.6 %copy-start.7 = (s32[4]{0:T(128)S(1)}, s32[4]{0:T(128)}, u32[]{:S(2)}) copy-start(s32[4]{0:T(128)} %refs_0_.15) | copy-start | bytes 52
  0.6 35.6 %copy-start.5 = (s32[4,4]{1,0:T(4,128)S(1)}, s32[4,4]{1,0:T(4,128)}, u32[]{:S(2)}) copy-start(s32[4,4]{1,0:T(4,128)} %refs_2_.7) | copy-start | bytes 196
  0.7 35.6 %copy-start.9 = (s32[4]{0:T(128)S(1)}, s32[4]{0:T(128)}, u32[]{:S(2)}) copy-start(s32[4]{0:T(128)} %refs_1_.7) | copy-start | bytes 52
  0.7 35.6 %copy-start.6 = (s32[4,4]{1,0:T(4,128)S(1)}, s32[4,4]{1,0:T(4,128)}, u32[]{:S(2)}) copy-start(s32[4,4]{1,0:T(4,128)} %refs_3_.7) | copy-start | bytes 196
  5.5 8.5 %collective-permute-start.20 = (f32[288,896]{1,0:T(8,128)}, f32[288,896]{1,0:T(8,128)S(1)}, u32[]{:S(2)}, u32[]{:S(2)}) collective-permute-start(f32[288,896]{1,0:T(8,128)} %get-tuple-element.123), channel_id=1, source_target_pairs={{8,16},{16,8},{9,17},{17,9},{10,18},{18,10},{11,19},{19,11},{12,20... | collective-permute-start | bytes 3096584 | tf_op jit(solution)/shard_map/ppermute | solution.py:597
  6.2 29.4 %collective-permute-start.14 = (f32[288,896]{1,0:T(8,128)}, f32[288,896]{1,0:T(8,128)S(1)}, u32[]{:S(2)}, u32[]{:S(2)}) collective-permute-start(f32[288,896]{1,0:T(8,128)} %get-tuple-element.115.refs_4_), channel_id=1, source_target_pairs={{0,8},{8,0},{16,24},{24,16},{1,9},{9,1},{17,25},{25,17},{2,10},{10... | collective-permute-start | bytes 3096584 | tf_op jit(solution)/shard_map/ppermute | solution.py:606
  12.1 45.7 %collective-permute-start.18 = (f32[288,896]{1,0:T(8,128)}, f32[288,896]{1,0:T(8,128)S(1)}, u32[]{:S(2)}, u32[]{:S(2)}) collective-permute-start(f32[288,896]{1,0:T(8,128)} %get-tuple-element.122), channel_id=1, source_target_pairs={{0,16},{24,8},{1,17},{25,9},{2,18},{26,10},{3,19},{27,11},{4,20},{... | collective-permute-start | bytes 3096584 | tf_op jit(solution)/shard_map/ppermute | solution.py:597
  13.9 45.1 %collective-permute-start.21 = (f32[288,896]{1,0:T(8,128)S(1)}, f32[288,896]{1,0:T(8,128)}, u32[]{:S(2)}, u32[]{:S(2)}) collective-permute-start(f32[288,896]{1,0:T(8,128)S(1)} %collective-permute-done.20.refs_7_), channel_id=1, source_target_pairs={{8,0},{16,24},{9,1},{17,25},{10,2},{18,26},{11,3},{19,27},{12,4},{... | collective-permute-start | bytes 3096584 | tf_op jit(solution)/shard_map/ppermute | solution.py:600
  40.8 76.6 %collective-permute-start.15 = (f32[288,896]{1,0:T(8,128)}, f32[288,896]{1,0:T(8,128)}, u32[]{:S(2)}, u32[]{:S(2)}) collective-permute-start(f32[288,896]{1,0:T(8,128)} %get-tuple-element.119), channel_id=1, source_target_pairs={{0,8},{24,16},{1,9},{25,17},{2,10},{26,18},{3,11},{27,19},{4,12},{... | collective-permute-start | bytes 3096584 | tf_op jit(solution)/shard_map/ppermute | solution.py:597
  46.0 71.3 %collective-permute-start.16 = (f32[288,896]{1,0:T(8,128)}, f32[288,896]{1,0:T(8,128)}, u32[]{:S(2)}, u32[]{:S(2)}) collective-permute-start(f32[288,896]{1,0:T(8,128)} %get-tuple-element.120), channel_id=1, source_target_pairs={{0,16},{24,8},{1,17},{25,9},{2,18},{26,10},{3,19},{27,11},{4,20},{... | collective-permute-start | bytes 3096584 | tf_op jit(solution)/shard_map/ppermute | solution.py:597
  48.3 69.1 %collective-permute-start.17 = (f32[288,896]{1,0:T(8,128)}, f32[288,896]{1,0:T(8,128)}, u32[]{:S(2)}, u32[]{:S(2)}) collective-permute-start(f32[288,896]{1,0:T(8,128)} %get-tuple-element.121), channel_id=1, source_target_pairs={{8,16},{16,8},{9,17},{17,9},{10,18},{18,10},{11,19},{19,11},{12,20... | collective-permute-start | bytes 3096584 | tf_op jit(solution)/shard_map/ppermute | solution.py:597
  57.8 23.9 %collective-permute-start.19 = (f32[288,896]{1,0:T(8,128)S(1)}, f32[288,896]{1,0:T(8,128)}, u32[]{:S(2)}, u32[]{:S(2)}) collective-permute-start(f32[288,896]{1,0:T(8,128)S(1)} %collective-permute-done.18.refs_6_), channel_id=1, source_target_pairs={{8,0},{16,24},{9,1},{17,25},{10,2},{18,26},{11,3},{19,27},{12,4},{... | collective-permute-start | bytes 3096584 | tf_op jit(solution)/shard_map/ppermute | solution.py:600
  61.0 73.8 %collective-permute-start.25 = (f32[288,896]{1,0:T(8,128)}, f32[288,896]{1,0:T(8,128)S(1)}, u32[]{:S(2)}, u32[]{:S(2)}) collective-permute-start(f32[288,896]{1,0:T(8,128)} %get-tuple-element.131), channel_id=1, source_target_pairs={{8,24},{16,0},{9,25},{17,1},{10,26},{18,2},{11,27},{19,3},{12,28},... | collective-permute-start | bytes 3096584 | tf_op jit(solution)/shard_map/ppermute | solution.py:600
  81.7 35.7 %copy-start.4 = (f32[288,896]{1,0:T(8,128)S(1)}, f32[288,896]{1,0:T(8,128)}, u32[]{:S(2)}) copy-start(f32[288,896]{1,0:T(8,128)} %get-tuple-element.118) | copy-start | bytes 3096580
  87.6 27.9 %copy-start.2 = (bf16[4,576,896]{2,1,0:T(8,128)(2,1)}, bf16[4,576,896]{2,1,0:T(8,128)(2,1)S(1)}, u32[]{:S(2)}) copy-start(bf16[4,576,896]{2,1,0:T(8,128)(2,1)S(1)} %get-tuple-element.144.refs_6_) | copy-start | bytes 12386308 | tf_op jit(solution)/shard_map/cond
  87.6 1.9 collective-permute-start
  89.5 8.4 %collective-permute-start.1 = (f32[288,384]{1,0:T(8,128)S(1)}, f32[288,384]{1,0:T(8,128)S(1)}, u32[]{:S(2)}, u32[]{:S(2)}) collective-permute-start(f32[288,384]{1,0:T(8,128)S(1)} %add.22), channel_id=1, source_target_pairs={{0,2},{1,5},{2,0},{3,7},{4,6},{5,1},{6,4},{7,3},{8,10},{9,13},{10,... | collective-permute-start | bytes 1327112 | tf_op jit(solution)/shard_map/cond/branch_0_fun/ppermute | solution.py:574
  97.9 8.4 %collective-permute-start.2 = (f32[288,384]{1,0:T(8,128)S(1)}, f32[288,384]{1,0:T(8,128)S(1)}, u32[]{:S(2)}, u32[]{:S(2)}) collective-permute-start(f32[288,384]{1,0:T(8,128)S(1)} %add.23), channel_id=1, source_target_pairs={{0,4},{1,3},{2,6},{3,1},{4,0},{5,7},{6,2},{7,5},{8,12},{9,11},{10,... | collective-permute-start | bytes 1327112 | tf_op jit(solution)/shard_map/cond/branch_0_fun/ppermute | solution.py:574
  106.4 1.9 collective-permute-start.3
  115.7 19.1 %collective-permute-start.26 = (f32[288,896]{1,0:T(8,128)}, f32[288,896]{1,0:T(8,128)}, u32[]{:S(2)}, u32[]{:S(2)}) collective-permute-start(f32[288,896]{1,0:T(8,128)} %get-tuple-element.132), channel_id=1, source_target_pairs={{8,16},{16,8},{9,17},{17,9},{10,18},{18,10},{11,19},{19,11},{12,20... | collective-permute-start | bytes 3096584 | tf_op jit(solution)/shard_map/ppermute | solution.py:600
  117.4 52.8 %collective-permute-start.24 = (f32[288,896]{1,0:T(8,128)}, f32[288,896]{1,0:T(8,128)S(1)}, u32[]{:S(2)}, u32[]{:S(2)}) collective-permute-start(f32[288,896]{1,0:T(8,128)} %get-tuple-element.127), channel_id=1, source_target_pairs={{8,24},{16,0},{9,25},{17,1},{10,26},{18,2},{11,27},{19,3},{12,28},... | collective-permute-start | bytes 3096584 | tf_op jit(solution)/shard_map/ppermute | solution.py:600
  118.7 72.6 %collective-permute-start.23 = (f32[288,896]{1,0:T(8,128)}, f32[288,896]{1,0:T(8,128)S(1)}, u32[]{:S(2)}, u32[]{:S(2)}) collective-permute-start(f32[288,896]{1,0:T(8,128)} %get-tuple-element.126), channel_id=1, source_target_pairs={{8,0},{16,24},{9,1},{17,25},{10,2},{18,26},{11,3},{19,27},{12,4},{... | collective-permute-start | bytes 3096584 | tf_op jit(solution)/shard_map/ppermute | solution.py:600
  120.0 72.8 %collective-permute-start.22 = (f32[288,896]{1,0:T(8,128)}, f32[288,896]{1,0:T(8,128)S(1)}, u32[]{:S(2)}, u32[]{:S(2)}) collective-permute-start(f32[288,896]{1,0:T(8,128)} %get-tuple-element.125), channel_id=1, source_target_pairs={{8,16},{16,8},{9,17},{17,9},{10,18},{18,10},{11,19},{19,11},{12,20... | collective-permute-start | bytes 3096584 | tf_op jit(solution)/shard_map/ppermute | solution.py:600
  127.4 7.4 %copy-start.8 = (s32[4]{0:T(128)S(1)}, s32[4]{0:T(128)}, u32[]{:S(2)}) copy-start(s32[4]{0:T(128)} %refs_0_.15) | copy-start | bytes 52
  (3 other events, 2.3 us)
where the time goes:
time: 194 us
  waiting for transfers between devices  117 us (60%)
  Pallas kernels  43.1 us (22%)
  starting transfers between devices  29.7 us (15%)
  local copies, waits for them, and re-layouts  2.31 us (1%)
    ppermute x7, waiting for transfers between devices, from_inner(): return lax.ppermute(block, 'fsdp', pairs(step, False))  71.6 us
    ppermute x1, waiting for transfers between devices, on_device(): swapped = lax.ppermute(own, 'fsdp', [(i, i ^ near) for i in range(ranks)])  20.4 us
    ppermute x4, waiting for transfers between devices, exchange(): lax.ppermute(piece, axis, [(i, i ^ bits[i & 1]) for i in range(size)])  17.2 us
    ppermute x5, starting transfers between devices, to_inner(): return lax.ppermute(block, 'fsdp', pairs(step, True))  11.7 us
    pallas_call x2, Pallas kernels, blend(): pl.pallas_call(functools.partial(blend_kernel, first, chunks), out_shape=...  9.32 us
    ppermute x7, starting transfers between devices, from_inner(): return lax.ppermute(block, 'fsdp', pairs(step, False))  8.81 us
    ppermute x5, waiting for transfers between devices, to_inner(): return lax.ppermute(block, 'fsdp', pairs(step, True))  7.86 us
    pallas_call x1, Pallas kernels, finish(): pl.pallas_call(functools.partial(finish_kernel, tables[1].shape[0]), out_...  7.38 us
  transfers between devices with their start and end apart: 17, of which 9 were waited for; matrix products, arithmetic and copies ran while one was open for 0% of the time, Pallas kernels for 19%

commit v1 on v0

--- a/solution.py
+++ b/solution.py
@@ -117,25 +117,25 @@
             getattr(pltpu.make_async_copy(source, place, flag), action)()
 
 
-def blend_kernel(first, chunks, *refs):
+def step_pairs(ranks):
+    outer = [step for step in range(1, ranks) if is_inner(step, ranks)]
+    inner = [step for step in range(1, ranks) if is_inner(mate(ranks) ^ step, ranks)]
+    return list(zip(outer, [*inner, 0]))
+
+
+def blend_kernel(first, steps, chunks, *refs):
     tables, (momentum, gradient) = refs[:4], refs[4:6]
     ranks = tables[1].shape[0]
-    *outs, token, olds, grads, arrive, leave = refs[-ranks - 10 + first : -5]
+    *outs, token, olds, grads, arrive, leave = refs[-len(steps) - 10 : -5]
     owner_group, live_ranks, row_counts, _ = fetch_tables(tables, refs[-5:])
     rank = lax.axis_index("fsdp")
     slots, columns = outs[0].shape
     size = slots // chunks
     jobs = []
-    for step in range(1, ranks + 1):
-        step = step % ranks
-        if first and step == 0:
-            continue
-        target = rank ^ step
-        wanted = is_inner(target, ranks)
+    for step, (outer, inner) in enumerate(steps):
+        target = rank ^ jnp.where(is_inner(rank, ranks), inner, outer)
+        wanted = rank >= 0
         matrix = matrix_of(owner_group, target ^ mate(ranks) if first else target)
-        if first and step == mate(ranks):
-            matrix = matrix_of(owner_group, jnp.where(wanted, rank, target))
-            wanted = rank >= 0
         count = row_counts[matrix, rank] * live_ranks[rank]
         for chunk in range(chunks):
             part = pl.ds(chunk * size, size)
@@ -144,7 +144,7 @@
                 (wanted, momentum.at[matrix, part], olds.at[step, part], flags[0]),
                 (wanted, gradient.at[matrix, part], grads.at[step, part], flags[1]),
             )
-            outgoing = (wanted, olds.at[step, part], outs[step - first].at[part], leave.at[step, chunk])
+            outgoing = (wanted, olds.at[step, part], outs[step].at[part], leave.at[step, chunk])
             jobs.append((step, chunk, count, incoming, outgoing))
             each_copy(incoming, "start")
     token[...] = jnp.zeros_like(token)
@@ -427,17 +427,16 @@
 FREE = pl.CostEstimate(flops=0, bytes_accessed=0, transcendentals=0)
 
 
-def blend(first, tables, momentum, gradient, before):
+def blend(first, steps, tables, momentum, gradient, before):
     _, slots, columns = momentum.shape
-    ranks = tables[1].shape[0]
     chunks = 2 if slots % (2 * SUBLANES) == 0 else 1
     return pl.pallas_call(
-        functools.partial(blend_kernel, first, chunks),
-        out_shape=[floats(slots, columns)] * (ranks - first) + [floats(SUBLANES, 128)],
+        functools.partial(blend_kernel, first, steps, chunks),
+        out_shape=[floats(slots, columns)] * len(steps) + [floats(SUBLANES, 128)],
         in_specs=[HBM] * 6 + [ANY] * len(before),
-        out_specs=[ANY] * (ranks - first) + [VMEM],
-        scratch_shapes=[vmem(ranks, slots, columns)] * 2
-        + [flags(ranks, chunks, 2), flags(ranks, chunks)]
+        out_specs=[ANY] * len(steps) + [VMEM],
+        scratch_shapes=[vmem(len(steps), slots, columns)] * 2
+        + [flags(len(steps), chunks, 2), flags(len(steps), chunks)]
         + table_scratch(*tables[2].shape),
         compiler_params=FULL,
         cost_estimate=FREE,
@@ -590,30 +589,39 @@
     last = [2, 1, *range(3, ranks)]
     early = [step for step in last if step != mate(ranks)]
 
-    def pairs(step, inward):
-        return [(i, i ^ step) for i in range(ranks) if is_inner(i ^ step if inward else i, ranks)]
-
-    def to_inner(block, step):
-        return lax.ppermute(block, "fsdp", pairs(step, True))
+    def passes(step, from_inside):
+        return [(i, i ^ step) for i in range(ranks) if is_inner(i, ranks) == from_inside]
+
+    def permute(block, pairs):
+        return lax.ppermute(block, "fsdp", pairs)
 
     def from_inner(block, step):
-        return lax.ppermute(block, "fsdp", pairs(step, False))
+        return permute(block, passes(step, True))
 
     near = mate(ranks)
+    steps = step_pairs(ranks)
+    arrived, last_arrived = {}, {}
+    *heads, token = blend(True, steps[:-1], tables, momentum, gradient, [])
+    for (outer_step, inner_step), block in zip(steps, heads):
+        arrived[outer_step] = permute(block, passes(outer_step, False))
+        arrived[inner_step] = from_inner(block, inner_step)
+    own, token = blend(True, steps[-1:], tables, momentum, gradient, [token])
+    swapped = permute(own, passes(steps[-1][0], False) + passes(near, True))
+    arrived[steps[-1][0]] = swapped
+    *blends, token = blend(False, steps, tables, momentum, gradient, [token, touch(arrived[near])])
+    for (outer_step, inner_step), block in zip(steps, blends):
+        last_arrived[outer_step] = permute(block, passes(outer_step, False))
+        if inner_step:
+            last_arrived[inner_step] = from_inner(block, inner_step)
+    last_blocks = [blends[-1]] + [last_arrived[step] for step in range(1, ranks)]
     far = [step for step in last if step != near]
-    *blends, token = blend(True, tables, momentum, gradient, [])
-    own = blends[near - 1]
-    swapped = lax.ppermute(own, "fsdp", [(i, i ^ near) for i in range(ranks)])
-    arrived = {step: to_inner(blends[step - 1], step) for step in far}
-    *blends, token = blend(False, tables, momentum, gradient, [token, touch(swapped)])
-    last_blocks = [blends[0]] + [to_inner(blends[step], step) for step in range(1, ranks)]
     new_momentum, token = fresh_momentum(tables, momentum, gradient, token)
     handed = {step: from_inner(arrived[step], near) for step in far}
 
     def ordered(base, opposite, others):
         return [{0: base, near: opposite, **others}[step] for step in range(ranks)]
 
-    first_blocks = ordered(own, swapped, arrived)
+    first_blocks = ordered(own, arrived[near], arrived)
     pair, keep, send = assemble_and_gram(True, True, tables, first_blocks, *[handed[step] for step in far[1:]])
 
     def first_update(pair, keep, send, after):
@@ -633,7 +641,7 @@
     def outer_skip(*_):
         return tuple(nothing([pair_shape, *update_shapes([], slots, columns)]))
 
-    outer_pair, outer_packed = lax.cond(inner, outer_skip, outer_update, *ordered(swapped, own, handed))
+    outer_pair, outer_packed = lax.cond(inner, outer_skip, outer_update, *ordered(swapped, heads[0], handed))
 
     def last_update(after, *blocks):
         pair, keep, send = assemble_and_gram(True, False, tables, blocks, after)

time: 194 us -> 195 us (level)
  waiting for transfers between devices: 117 us -> 114 us
  Pallas kernels: 43.1 us -> 45.4 us
    ppermute x13, waiting for transfers between devices: 99.9 us -> 97.2 us  [permute(): return lax.ppermute(block, 'fsdp', pairs)]
    pallas_call x2 -> x3, Pallas kernels: 9.32 us -> 11.9 us  [blend(): pl.pallas_call(functools.partial(blend_kernel, first, steps, chunks), out...]
  transfers between devices with their start and end apart: 17 -> 17, of which waited for: 9 -> 10; matrix products, arithmetic and copies ran while one was open for 0% -> 0% of each run, Pallas kernels for 19% -> 21%
where the time goes in v1:
time: 195 us
  waiting for transfers between devices  114 us (58%)
  Pallas kernels  45.4 us (23%)
  starting transfers between devices  30.8 us (16%)
  local copies, waits for them, and re-layouts  2.33 us (1%)
    ppermute x13, waiting for transfers between devices, permute(): return lax.ppermute(block, 'fsdp', pairs)  97.2 us
    ppermute x13, starting transfers between devices, permute(): return lax.ppermute(block, 'fsdp', pairs)  27.5 us
    ppermute x4, waiting for transfers between devices, exchange(): lax.ppermute(piece, axis, [(i, i ^ bits[i & 1]) for i in range(size)])  17.2 us
    pallas_call x3, Pallas kernels, blend(): pl.pallas_call(functools.partial(blend_kernel, first, steps, chunks), out...  11.9 us
    pallas_call x1, Pallas kernels, finish(): pl.pallas_call(functools.partial(finish_kernel, tables[1].shape[0]), out_...  7.38 us
    pallas_call x1, Pallas kernels, apply_update(): pl.pallas_call(functools.partial(update_kernel, first, steps), out_shape=...  7.27 us
    pallas_call x2, Pallas kernels, assemble_and_gram(): pl.pallas_call(functools.partial(gram_kernel, inner, first, ranks), out_s...  6.56 us
    pallas_call x4, Pallas kernels, place_blocks(): pl.pallas_call(functools.partial(place_kernel, first, ranks, steps), out_...  6.37 us
  transfers between devices with their start and end apart: 17, of which 10 were waited for; matrix products, arithmetic and copies ran while one was open for 0% of the time, Pallas kernels for 21%

profile of v1, /device:TPU:0, one launch (start us, length us, event | category | flops | bytes accessed | tf_op | source)
XLA Modules:
  0.0 194.5 jit_solution(15910125727193799150)
XLA Ops:
  0.7 3.8 %blend.3 = (f32[288,896]{1,0:T(8,128)S(1)}, f32[8,128]{1,0:T(8,128)}) custom-call(s32[4]{0:T(128)} %refs_0_.17, s32[4]{0:T(128)} %refs_1_.9, s32[4,4]{1,0:T(4,128)} %refs_2_.9, s32[4,4]{1,0:T(4,128)} %refs_3_.9, f32[4,288,896]{2,1,0:T(8,128)} %momentum.1, f32[4,288,896]{2,1,0:T(8,128)} %gradient.1), custom_call_target="tpu_custom_call" | custom-call | tf_op jit(solution)/shard_map/blend/pallas_call | solution.py:433
  5.2 7.8 %collective-permute-start.14 = (f32[288,896]{1,0:T(8,128)S(1)}, f32[288,896]{1,0:T(8,128)S(1)}, u32[]{:S(2)}, u32[]{:S(2)}) collective-permute-start(f32[288,896]{1,0:T(8,128)S(1)} %get-tuple-element.114), channel_id=1, source_target_pairs={{0,8},{24,16},{1,9},{25,17},{2,10},{26,18},{3,11},{27,19},{4,12},{... | collective-permute-start | bytes 3096584 | tf_op jit(solution)/shard_map/ppermute | solution.py:596
  13.0 3.7 %blend.4 = (f32[288,896]{1,0:T(8,128)}, f32[8,128]{1,0:T(8,128)}) custom-call(s32[4]{0:T(128)S(1)} %copy-done.10, s32[4]{0:T(128)S(1)} %copy-done.12, s32[4,4]{1,0:T(4,128)S(1)} %copy-done.8, s32[4,4]{1,0:T(4,128)S(1)} %copy-done.9, f32[4,288,896]{2,1,0:T(8,128)} %momentum.1, f32[4,288,896]{2,1,0:T(8,128)} %gradient.1, f32[8,128]{1,0:T(8,128)} %get-tuple-element.112.refs_6_), custom_call_target="tpu_custom_call" | custom-call | tf_op jit(solution)/shard_map/blend/pallas_call | solution.py:433
  18.1 18.0 %collective-permute-done.14.refs_0_.refs_5_ = f32[288,896]{1,0:T(8,128)S(1)} collective-permute-done((f32[288,896]{1,0:T(8,128)S(1)}, f32[288,896]{1,0:T(8,128)S(1)}, u32[]{:S(2)}, u32[]{:S(2)}) %collective-permute-start.14) | collective-permute-done | bytes 1032224 | tf_op jit(solution)/shard_map/ppermute | solution.py:596
  36.7 4.4 %blend.5 = (f32[288,896]{1,0:T(8,128)}, f32[288,896]{1,0:T(8,128)}, f32[8,128]{1,0:T(8,128)}) custom-call(s32[4]{0:T(128)S(1)} %copy-done.10, s32[4]{0:T(128)S(1)} %copy-done.12, s32[4,4]{1,0:T(4,128)S(1)} %copy-done.8, s32[4,4]{1,0:T(4,128)S(1)} %copy-done.9, f32[4,288,896]{2,1,0:T(8,128)} %momentum.1, f32[4,288,896]{2,1,0:T(8,128)} %gradient.1, ...), custom_call_target="tpu_custom_call" | custom-call | tf_op jit(solution)/shard_map/blend/pallas_call | solution.py:433
  41.1 1.7 collective-permute-start.17
  42.8 6.0 %collective-permute-start.15 = (f32[288,896]{1,0:T(8,128)}, f32[288,896]{1,0:T(8,128)}, u32[]{:S(2)}, u32[]{:S(2)}) collective-permute-start(f32[288,896]{1,0:T(8,128)} %get-tuple-element.118), channel_id=1, source_target_pairs={{0,8},{24,16},{1,9},{25,17},{2,10},{26,18},{3,11},{27,19},{4,12},{... | collective-permute-start | bytes 3096584 | tf_op jit(solution)/shard_map/ppermute | solution.py:596
  48.9 2.3 %collective-permute-start.16 = (f32[288,896]{1,0:T(8,128)}, f32[288,896]{1,0:T(8,128)}, u32[]{:S(2)}, u32[]{:S(2)}) collective-permute-start(f32[288,896]{1,0:T(8,128)} %get-tuple-element.117), channel_id=1, source_target_pairs={{0,16},{24,8},{1,17},{25,9},{2,18},{26,10},{3,19},{27,11},{4,20},{... | collective-permute-start | bytes 3096584 | tf_op jit(solution)/shard_map/ppermute | solution.py:596
  51.2 7.2 %collective-permute-done.18.refs_6_ = f32[288,896]{1,0:T(8,128)} collective-permute-done((f32[288,896]{1,0:T(8,128)}, f32[288,896]{1,0:T(8,128)}, u32[]{:S(2)}, u32[]{:S(2)}) %collective-permute-start.18) | collective-permute-done | bytes 1032224 | tf_op jit(solution)/shard_map/ppermute | solution.py:596
  59.7 5.3 %collective-permute-done.21.refs_8_ = f32[288,896]{1,0:T(8,128)} collective-permute-done((f32[288,896]{1,0:T(8,128)S(1)}, f32[288,896]{1,0:T(8,128)}, u32[]{:S(2)}, u32[]{:S(2)}) %collective-permute-start.21) | collective-permute-done | bytes 1032224 | tf_op jit(solution)/shard_map/ppermute | solution.py:596
  68.3 17.1 %collective-permute-done.19 = f32[288,896]{1,0:T(8,128)} collective-permute-done((f32[288,896]{1,0:T(8,128)}, f32[288,896]{1,0:T(8,128)}, u32[]{:S(2)}, u32[]{:S(2)}) %collective-permute-start.19) | collective-permute-done | bytes 1032224 | tf_op jit(solution)/shard_map/ppermute | solution.py:596
  85.4 33.8 %conditional.3 = ((bf16[4,576,896]{2,1,0:T(8,128)(2,1)}, f32[576,384]{1,0:T(8,128)})) conditional(s32[]{:T(128)} %convert_element_type.2, (s32[4]{0:T(128)S(1)}, s32[4]{0:T(128)S(1)}, s32[4,4]{1,0:T(4,128)S(1)}, s32[4,4]{1,0:T(4,128)S(1)}, f32[288,896]{1,0:T(8,128)}, /*index=5*/f32[288,896]{1,0:T(8,128)S(1)}, f32[288,896]{1,0:T(8,128)}, ...), branch_computations={%region_0.0_spmd, %region_1.0_spmd} | conditional | flops 331776 | bytes 27574484 | solution.py:644
  85.4 5.7 %assemble_and_gram.3 = (bf16[4,576,896]{2,1,0:T(8,128)(2,1)S(1)}, f32[288,384]{1,0:T(8,128)S(1)}, f32[288,384]{1,0:T(8,128)S(1)}) custom-call(s32[4]{0:T(128)S(1)} %get-tuple-element.50.refs_0_, s32[4]{0:T(128)S(1)} %get-tuple-element.51.refs_1_, s32[4,4]{1,0:T(4,128)S(1)} %get-tuple-element.52.refs_2_, s32[4,4]{1,0:T(4,128)S(1)} %get-tuple-element.53.refs_3_, ...), custom_call_target="tpu_custom_call" | custom-call | tf_op jit(solution)/shard_map/cond/branch_0_fun/assemble_and_gram/pallas_call | solution.py:466
  91.2 1.8 collective-permute-done
  94.5 6.8 %collective-permute-done.1 = f32[288,384]{1,0:T(8,128)S(1)} collective-permute-done((f32[288,384]{1,0:T(8,128)S(1)}, f32[288,384]{1,0:T(8,128)S(1)}, u32[]{:S(2)}, u32[]{:S(2)}) %collective-permute-start.1) | collective-permute-done | bytes 442400 | tf_op jit(solution)/shard_map/cond/branch_0_fun/ppermute | solution.py:573
  103.0 6.8 %collective-permute-done.2 = f32[288,384]{1,0:T(8,128)S(1)} collective-permute-done((f32[288,384]{1,0:T(8,128)S(1)}, f32[288,384]{1,0:T(8,128)S(1)}, u32[]{:S(2)}, u32[]{:S(2)}) %collective-permute-start.2) | collective-permute-done | bytes 442400 | tf_op jit(solution)/shard_map/cond/branch_0_fun/ppermute | solution.py:573
  109.9 1.8 collective-permute-done.3.refs_5_
  111.7 7.3 %apply_update.3 = f32[576,384]{1,0:T(8,128)} custom-call(s32[4]{0:T(128)S(1)} %get-tuple-element.50.refs_0_, s32[4]{0:T(128)S(1)} %get-tuple-element.51.refs_1_, s32[4,4]{1,0:T(4,128)S(1)} %get-tuple-element.52.refs_2_, s32[4,4]{1,0:T(4,128)S(1)} %get-tuple-element.53.refs_3_, f32[288,384]{1,0:T(8,128)S(1)} %add.24.refs_4_, ...), custom_call_target="tpu_custom_call" | custom-call | tf_op jit(solution)/shard_map/cond/branch_0_fun/apply_update/pallas_call | solution.py:499
  119.2 1.6 collective-permute-start.26
  124.2 5.9 %fresh_momentum.1 = (f32[4,288,896]{2,1,0:T(8,128)}, f32[8,128]{1,0:T(8,128)}) custom-call(s32[4]{0:T(128)} %refs_1_.9, s32[4,4]{1,0:T(4,128)} %refs_2_.9, f32[4,288,896]{2,1,0:T(8,128)} %momentum.1, f32[4,288,896]{2,1,0:T(8,128)} %gradient.1, f32[8,128]{1,0:T(8,128)} %get-tuple-element.115._), custom_call_target="tpu_custom_call" | custom-call | tf_op jit(solution)/shard_map/fresh_momentum/pallas_call | solution.py:450
  130.9 7.4 %finish.1 = (f32[576,896]{1,0:T(8,128)}, f32[4,288,896]{2,1,0:T(8,128)}) custom-call(s32[4]{0:T(128)} %refs_0_.17, s32[4]{0:T(128)} %refs_1_.9, s32[4,4]{1,0:T(4,128)} %refs_2_.9, s32[4,4]{1,0:T(4,128)} %refs_3_.9, f32[576,384]{1,0:T(8,128)} %get-tuple-element.129.refs_4_, bf16[4,576,896]{2,1,0:T(8,128)(2,1)} %get-tuple-element.126.refs_5_, ...), custom_call_target="tpu_custom_call" | custom-call | tf_op jit(solution)/shard_map/finish/pallas_call | solution.py:534
  138.3 2.8 %place_blocks.4.refs_2_ = f32[4,288,896]{2,1,0:T(8,128)} custom-call(s32[4]{0:T(128)S(1)} %copy-done.11, f32[288,896]{1,0:T(8,128)S(1)} %collective-permute-done.25.refs_1_, f32[288,896]{1,0:T(8,128)} %collective-permute-done.26.refs_2_, f32[4,288,896]{2,1,0:T(8,128)} %get-tuple-element.134.refs_3_), custom_call_target="tpu_custom_call", output_to_operand_aliasing={{}: (3, {})} | custom-call | tf_op jit(solution)/shard_map/place_blocks/pallas_call | solution.py:556
  141.0 30.1 %collective-permute-done.24.refs_1_ = f32[288,896]{1,0:T(8,128)S(1)} collective-permute-done((f32[288,896]{1,0:T(8,128)}, f32[288,896]{1,0:T(8,128)S(1)}, u32[]{:S(2)}, u32[]{:S(2)}) %collective-permute-start.24) | collective-permute-done | bytes 1032224 | tf_op jit(solution)/shard_map/ppermute | solution.py:596
  172.6 19.6 %collective-permute-done.23.refs_1_ = f32[288,896]{1,0:T(8,128)S(1)} collective-permute-done((f32[288,896]{1,0:T(8,128)}, f32[288,896]{1,0:T(8,128)S(1)}, u32[]{:S(2)}, u32[]{:S(2)}) %collective-permute-start.23) | collective-permute-done | bytes 1032224 | tf_op jit(solution)/shard_map/ppermute | solution.py:596
  (58 shorter events, 18.3 us)
Async XLA Ops:
  0.6 12.3 %copy-start.10 = (s32[4]{0:T(128)S(1)}, s32[4]{0:T(128)}, u32[]{:S(2)}) copy-start(s32[4]{0:T(128)} %refs_0_.17) | copy-start | bytes 52
  0.6 12.3 %copy-start.8 = (s32[4,4]{1,0:T(4,128)S(1)}, s32[4,4]{1,0:T(4,128)}, u32[]{:S(2)}) copy-start(s32[4,4]{1,0:T(4,128)} %refs_2_.9) | copy-start | bytes 196
  0.7 12.3 %copy-start.12 = (s32[4]{0:T(128)S(1)}, s32[4]{0:T(128)}, u32[]{:S(2)}) copy-start(s32[4]{0:T(128)} %refs_1_.9) | copy-start | bytes 52
  4.5 12.4 %collective-permute-start.20 = (f32[288,896]{1,0:T(8,128)S(1)}, f32[288,896]{1,0:T(8,128)S(1)}, u32[]{:S(2)}, u32[]{:S(2)}) collective-permute-start(f32[288,896]{1,0:T(8,128)S(1)} %get-tuple-element.114), channel_id=1, source_target_pairs={{8,16},{16,8},{9,17},{17,9},{10,18},{18,10},{11,19},{19,11},{12,20... | collective-permute-start | bytes 3096584 | tf_op jit(solution)/shard_map/ppermute | solution.py:596
  5.2 30.9 %collective-permute-start.14 = (f32[288,896]{1,0:T(8,128)S(1)}, f32[288,896]{1,0:T(8,128)S(1)}, u32[]{:S(2)}, u32[]{:S(2)}) collective-permute-start(f32[288,896]{1,0:T(8,128)S(1)} %get-tuple-element.114), channel_id=1, source_target_pairs={{0,8},{24,16},{1,9},{25,17},{2,10},{26,18},{3,11},{27,19},{4,12},{... | collective-permute-start | bytes 3096584 | tf_op jit(solution)/shard_map/ppermute | solution.py:596
  16.8 41.6 %collective-permute-start.18 = (f32[288,896]{1,0:T(8,128)}, f32[288,896]{1,0:T(8,128)}, u32[]{:S(2)}, u32[]{:S(2)}) collective-permute-start(f32[288,896]{1,0:T(8,128)} %get-tuple-element.119.refs_4_), channel_id=1, source_target_pairs={{0,16},{24,8},{8,0},{16,24},{1,17},{25,9},{9,1},{17,25},{2,18},{26... | collective-permute-start | bytes 3096584 | tf_op jit(solution)/shard_map/ppermute | solution.py:596
  16.8 48.2 %collective-permute-start.21 = (f32[288,896]{1,0:T(8,128)S(1)}, f32[288,896]{1,0:T(8,128)}, u32[]{:S(2)}, u32[]{:S(2)}) collective-permute-start(f32[288,896]{1,0:T(8,128)S(1)} %collective-permute-done.20.refs_7_), channel_id=1, source_target_pairs={{8,0},{16,24},{9,1},{17,25},{10,2},{18,26},{11,3},{19,27},{12,4},{... | collective-permute-start | bytes 3096584 | tf_op jit(solution)/shard_map/ppermute | solution.py:596
  36.7 28.3 %copy-start = (f32[288,896]{1,0:T(8,128)S(1)}, f32[288,896]{1,0:T(8,128)}, u32[]{:S(2)}) copy-start(f32[288,896]{1,0:T(8,128)} %get-tuple-element.119.refs_4_) | copy-start | bytes 3096580
  41.1 79.7 %collective-permute-start.17 = (f32[288,896]{1,0:T(8,128)}, f32[288,896]{1,0:T(8,128)}, u32[]{:S(2)}, u32[]{:S(2)}) collective-permute-start(f32[288,896]{1,0:T(8,128)} %get-tuple-element.118), channel_id=1, source_target_pairs={{8,16},{16,8},{9,17},{17,9},{10,18},{18,10},{11,19},{19,11},{12,20... | collective-permute-start | bytes 3096584 | tf_op jit(solution)/shard_map/ppermute | solution.py:596
  42.8 78.0 %collective-permute-start.15 = (f32[288,896]{1,0:T(8,128)}, f32[288,896]{1,0:T(8,128)}, u32[]{:S(2)}, u32[]{:S(2)}) collective-permute-start(f32[288,896]{1,0:T(8,128)} %get-tuple-element.118), channel_id=1, source_target_pairs={{0,8},{24,16},{1,9},{25,17},{2,10},{26,18},{3,11},{27,19},{4,12},{... | collective-permute-start | bytes 3096584 | tf_op jit(solution)/shard_map/ppermute | solution.py:596
  48.9 72.0 %collective-permute-start.16 = (f32[288,896]{1,0:T(8,128)}, f32[288,896]{1,0:T(8,128)}, u32[]{:S(2)}, u32[]{:S(2)}) collective-permute-start(f32[288,896]{1,0:T(8,128)} %get-tuple-element.117), channel_id=1, source_target_pairs={{0,16},{24,8},{1,17},{25,9},{2,18},{26,10},{3,19},{27,11},{4,20},{... | collective-permute-start | bytes 3096584 | tf_op jit(solution)/shard_map/ppermute | solution.py:596
  58.4 27.0 %collective-permute-start.19 = (f32[288,896]{1,0:T(8,128)}, f32[288,896]{1,0:T(8,128)}, u32[]{:S(2)}, u32[]{:S(2)}) collective-permute-start(f32[288,896]{1,0:T(8,128)} %collective-permute-done.18.refs_6_), channel_id=1, source_target_pairs={{8,0},{16,24},{9,1},{17,25},{10,2},{18,26},{11,3},{19,27},{12,4},{... | collective-permute-start | bytes 3096584 | tf_op jit(solution)/shard_map/ppermute | solution.py:596
  66.9 18.5 %copy-start.7 = (f32[288,896]{1,0:T(8,128)S(1)}, f32[288,896]{1,0:T(8,128)}, u32[]{:S(2)}) copy-start(f32[288,896]{1,0:T(8,128)} %copy-done.6) | copy-start | bytes 3096580
  66.9 71.4 %collective-permute-start.25 = (f32[288,896]{1,0:T(8,128)}, f32[288,896]{1,0:T(8,128)S(1)}, u32[]{:S(2)}, u32[]{:S(2)}) collective-permute-start(f32[288,896]{1,0:T(8,128)} %get-tuple-element.127), channel_id=1, source_target_pairs={{8,24},{16,0},{9,25},{17,1},{10,26},{18,2},{11,27},{19,3},{12,28},... | collective-permute-start | bytes 3096584 | tf_op jit(solution)/shard_map/ppermute | solution.py:596
  85.4 35.5 %copy-start.5 = (f32[288,896]{1,0:T(8,128)S(1)}, f32[288,896]{1,0:T(8,128)}, u32[]{:S(2)}) copy-start(f32[288,896]{1,0:T(8,128)} %get-tuple-element.117) | copy-start | bytes 3096580
  91.1 27.9 %copy-start.3 = (bf16[4,576,896]{2,1,0:T(8,128)(2,1)}, bf16[4,576,896]{2,1,0:T(8,128)(2,1)S(1)}, u32[]{:S(2)}) copy-start(bf16[4,576,896]{2,1,0:T(8,128)(2,1)S(1)} %get-tuple-element.140.refs_6_) | copy-start | bytes 12386308 | tf_op jit(solution)/shard_map/cond
  91.1 1.9 collective-permute-start
  93.0 8.4 %collective-permute-start.1 = (f32[288,384]{1,0:T(8,128)S(1)}, f32[288,384]{1,0:T(8,128)S(1)}, u32[]{:S(2)}, u32[]{:S(2)}) collective-permute-start(f32[288,384]{1,0:T(8,128)S(1)} %add.22), channel_id=1, source_target_pairs={{0,2},{1,5},{2,0},{3,7},{4,6},{5,1},{6,4},{7,3},{8,10},{9,13},{10,... | collective-permute-start | bytes 1327112 | tf_op jit(solution)/shard_map/cond/branch_0_fun/ppermute | solution.py:573
  101.4 8.4 %collective-permute-start.2 = (f32[288,384]{1,0:T(8,128)S(1)}, f32[288,384]{1,0:T(8,128)S(1)}, u32[]{:S(2)}, u32[]{:S(2)}) collective-permute-start(f32[288,384]{1,0:T(8,128)S(1)} %add.23), channel_id=1, source_target_pairs={{0,4},{1,3},{2,6},{3,1},{4,0},{5,7},{6,2},{7,5},{8,12},{9,11},{10,... | collective-permute-start | bytes 1327112 | tf_op jit(solution)/shard_map/cond/branch_0_fun/ppermute | solution.py:573
  109.8 1.9 collective-permute-start.3
  119.2 19.1 %collective-permute-start.26 = (f32[288,896]{1,0:T(8,128)}, f32[288,896]{1,0:T(8,128)}, u32[]{:S(2)}, u32[]{:S(2)}) collective-permute-start(f32[288,896]{1,0:T(8,128)} %get-tuple-element.128), channel_id=1, source_target_pairs={{8,16},{16,8},{9,17},{17,9},{10,18},{18,10},{11,19},{19,11},{12,20... | collective-permute-start | bytes 3096584 | tf_op jit(solution)/shard_map/ppermute | solution.py:596
  120.9 50.2 %collective-permute-start.24 = (f32[288,896]{1,0:T(8,128)}, f32[288,896]{1,0:T(8,128)S(1)}, u32[]{:S(2)}, u32[]{:S(2)}) collective-permute-start(f32[288,896]{1,0:T(8,128)} %get-tuple-element.123), channel_id=1, source_target_pairs={{8,24},{16,0},{9,25},{17,1},{10,26},{18,2},{11,27},{19,3},{12,28},... | collective-permute-start | bytes 3096584 | tf_op jit(solution)/shard_map/ppermute | solution.py:596
  122.2 70.0 %collective-permute-start.23 = (f32[288,896]{1,0:T(8,128)}, f32[288,896]{1,0:T(8,128)S(1)}, u32[]{:S(2)}, u32[]{:S(2)}) collective-permute-start(f32[288,896]{1,0:T(8,128)} %get-tuple-element.122), channel_id=1, source_target_pairs={{8,0},{16,24},{9,1},{17,25},{10,2},{18,26},{11,3},{19,27},{12,4},{... | collective-permute-start | bytes 3096584 | tf_op jit(solution)/shard_map/ppermute | solution.py:596
  123.5 70.3 %collective-permute-start.22 = (f32[288,896]{1,0:T(8,128)}, f32[288,896]{1,0:T(8,128)S(1)}, u32[]{:S(2)}, u32[]{:S(2)}) collective-permute-start(f32[288,896]{1,0:T(8,128)} %get-tuple-element.121), channel_id=1, source_target_pairs={{8,16},{16,8},{9,17},{17,9},{10,18},{18,10},{11,19},{19,11},{12,20... | collective-permute-start | bytes 3096584 | tf_op jit(solution)/shard_map/ppermute | solution.py:596
  (6 other events, 34.3 us)

commit v2 on v0

--- a/solution.py
+++ b/solution.py
@@ -648,8 +648,8 @@
     sources = [packed, pair, last_packed, last_pair, outer_packed, outer_pair]
     result, shards = finish(tables, sources, momentum.shape, token)
     shards = place_blocks(True, owner_group, early, first_home, shards, ranks)
-    for step, block in zip(last, last_home):
-        shards = place_blocks(False, owner_group, [step], [block], shards, ranks)
+    shards = place_blocks(False, owner_group, last[:1], last_home[:1], shards, ranks)
+    shards = place_blocks(False, owner_group, last[1:], last_home[1:], shards, ranks)
     return (new_momentum, shards, result[None])
 
 

time: 194 us -> 195 us (level)
  waiting for transfers between devices: 117 us -> 119 us
    pallas_call x4 -> x3, Pallas kernels: 6.37 us -> 6.12 us  [place_blocks(): pl.pallas_call(functools.partial(place_kernel, first, ranks, steps), out_...]
  transfers between devices with their start and end apart: 17 -> 17, of which waited for: 9 -> 9; matrix products, arithmetic and copies ran while one was open for 0% -> 0% of each run, Pallas kernels for 19% -> 18%
where the time goes in v2:
time: 195 us
  waiting for transfers between devices  119 us (61%)
  Pallas kernels  42.5 us (22%)
  starting transfers between devices  29.7 us (15%)
  local copies, waits for them, and re-layouts  2.29 us (1%)
    ppermute x7, waiting for transfers between devices, from_inner(): return lax.ppermute(block, 'fsdp', pairs(step, False))  73.1 us
    ppermute x1, waiting for transfers between devices, on_device(): swapped = lax.ppermute(own, 'fsdp', [(i, i ^ near) for i in range(ranks)])  20.4 us
    ppermute x4, waiting for transfers between devices, exchange(): lax.ppermute(piece, axis, [(i, i ^ bits[i & 1]) for i in range(size)])  17.2 us
    ppermute x5, starting transfers between devices, to_inner(): return lax.ppermute(block, 'fsdp', pairs(step, True))  11.8 us
    pallas_call x2, Pallas kernels, blend(): pl.pallas_call(functools.partial(blend_kernel, first, chunks), out_shape=...  9.33 us
    ppermute x7, starting transfers between devices, from_inner(): return lax.ppermute(block, 'fsdp', pairs(step, False))  8.83 us
    ppermute x5, waiting for transfers between devices, to_inner(): return lax.ppermute(block, 'fsdp', pairs(step, True))  7.85 us
    pallas_call x1, Pallas kernels, apply_update(): pl.pallas_call(functools.partial(update_kernel, first, steps), out_shape=...  7.25 us
  transfers between devices with their start and end apart: 17, of which 9 were waited for; matrix products, arithmetic and copies ran while one was open for 0% of the time, Pallas kernels for 18%

profile of v2, /device:TPU:0, one launch (start us, length us, event | category | flops | bytes accessed | tf_op | source)
XLA Modules:
  0.0 194.6 jit_solution(17309980192395599262)
XLA Ops:
  0.7 4.8 %blend.2 = (f32[288,896]{1,0:T(8,128)}, f32[288,896]{1,0:T(8,128)}, f32[288,896]{1,0:T(8,128)}, f32[8,128]{1,0:T(8,128)}) custom-call(s32[4]{0:T(128)} %refs_0_.13, s32[4]{0:T(128)} %refs_1_.7, s32[4,4]{1,0:T(4,128)} %refs_2_.7, s32[4,4]{1,0:T(4,128)} %refs_3_.7, f32[4,288,896]{2,1,0:T(8,128)} %momentum.1, f32[4,288,896]{2,1,0:T(8,128)} %gradient.1), custom_call_target="tpu_custom_call" | custom-call | tf_op jit(solution)/shard_map/blend/pallas_call | solution.py:434
  6.2 5.8 %collective-permute-start.14 = (f32[288,896]{1,0:T(8,128)}, f32[288,896]{1,0:T(8,128)S(1)}, u32[]{:S(2)}, u32[]{:S(2)}) collective-permute-start(f32[288,896]{1,0:T(8,128)} %get-tuple-element.115.refs_4_), channel_id=1, source_target_pairs={{0,8},{8,0},{16,24},{24,16},{1,9},{9,1},{17,25},{25,17},{2,10},{10... | collective-permute-start | bytes 3096584 | tf_op jit(solution)/shard_map/ppermute | solution.py:606
  12.0 1.9 collective-permute-start.18
  15.2 20.4 %collective-permute-done.14.refs_0_.refs_5_ = f32[288,896]{1,0:T(8,128)S(1)} collective-permute-done((f32[288,896]{1,0:T(8,128)}, f32[288,896]{1,0:T(8,128)S(1)}, u32[]{:S(2)}, u32[]{:S(2)}) %collective-permute-start.14) | collective-permute-done | bytes 1032224 | tf_op jit(solution)/shard_map/ppermute | solution.py:606
  36.2 4.5 %blend.3 = (f32[288,896]{1,0:T(8,128)}, f32[288,896]{1,0:T(8,128)}, f32[288,896]{1,0:T(8,128)}, f32[288,896]{1,0:T(8,128)}, f32[8,128]{1,0:T(8,128)}) custom-call(s32[4]{0:T(128)S(1)} %copy-done.7, s32[4]{0:T(128)S(1)} %copy-done.8, s32[4,4]{1,0:T(4,128)S(1)} %copy-done.5, s32[4,4]{1,0:T(4,128)S(1)} %copy-done.6, f32[4,288,896]{2,1,0:T(8,128)} %momentum.1, ...), custom_call_target="tpu_custom_call" | custom-call | tf_op jit(solution)/shard_map/blend/pallas_call | solution.py:434
  40.8 5.3 %collective-permute-start.15 = (f32[288,896]{1,0:T(8,128)}, f32[288,896]{1,0:T(8,128)}, u32[]{:S(2)}, u32[]{:S(2)}) collective-permute-start(f32[288,896]{1,0:T(8,128)} %get-tuple-element.119), channel_id=1, source_target_pairs={{0,8},{24,16},{1,9},{25,17},{2,10},{26,18},{3,11},{27,19},{4,12},{... | collective-permute-start | bytes 3096584 | tf_op jit(solution)/shard_map/ppermute | solution.py:597
  46.0 2.3 %collective-permute-start.16 = (f32[288,896]{1,0:T(8,128)}, f32[288,896]{1,0:T(8,128)}, u32[]{:S(2)}, u32[]{:S(2)}) collective-permute-start(f32[288,896]{1,0:T(8,128)} %get-tuple-element.120), channel_id=1, source_target_pairs={{0,16},{24,8},{1,17},{25,9},{2,18},{26,10},{3,19},{27,11},{4,20},{... | collective-permute-start | bytes 3096584 | tf_op jit(solution)/shard_map/ppermute | solution.py:597
  48.3 1.6 collective-permute-start.17
  49.9 7.8 %collective-permute-done.18.refs_6_ = f32[288,896]{1,0:T(8,128)S(1)} collective-permute-done((f32[288,896]{1,0:T(8,128)}, f32[288,896]{1,0:T(8,128)S(1)}, u32[]{:S(2)}, u32[]{:S(2)}) %collective-permute-start.18) | collective-permute-done | bytes 1032224 | tf_op jit(solution)/shard_map/ppermute | solution.py:597
  62.3 19.4 %collective-permute-done.19 = f32[288,896]{1,0:T(8,128)} collective-permute-done((f32[288,896]{1,0:T(8,128)S(1)}, f32[288,896]{1,0:T(8,128)}, u32[]{:S(2)}, u32[]{:S(2)}) %collective-permute-start.19) | collective-permute-done | bytes 1032224 | tf_op jit(solution)/shard_map/ppermute | solution.py:600
  81.7 34.0 %conditional.3 = ((bf16[4,576,896]{2,1,0:T(8,128)(2,1)}, f32[576,384]{1,0:T(8,128)})) conditional(s32[]{:T(128)} %convert_element_type.2, (s32[4]{0:T(128)S(1)}, s32[4]{0:T(128)S(1)}, s32[4,4]{1,0:T(4,128)S(1)}, s32[4,4]{1,0:T(4,128)S(1)}, f32[288,896]{1,0:T(8,128)S(1)}, /*index=5*/f32[288,896]{1,0:T(8,128)}, f32[288,896]{1,0:T(8,128)}, ...), branch_computations={%region_0.0_spmd, %region_1.0_spmd} | conditional | flops 331776 | bytes 27574484 | solution.py:636
  81.7 5.9 %assemble_and_gram.3 = (bf16[4,576,896]{2,1,0:T(8,128)(2,1)S(1)}, f32[288,384]{1,0:T(8,128)S(1)}, f32[288,384]{1,0:T(8,128)S(1)}) custom-call(s32[4]{0:T(128)S(1)} %get-tuple-element.50.refs_0_, s32[4]{0:T(128)S(1)} %get-tuple-element.51.refs_1_, s32[4,4]{1,0:T(4,128)S(1)} %get-tuple-element.52.refs_2_, s32[4,4]{1,0:T(4,128)S(1)} %get-tuple-element.53.refs_3_, ...), custom_call_target="tpu_custom_call" | custom-call | tf_op jit(solution)/shard_map/cond/branch_0_fun/assemble_and_gram/pallas_call | solution.py:467
  87.7 1.8 collective-permute-done
  91.1 6.8 %collective-permute-done.1 = f32[288,384]{1,0:T(8,128)S(1)} collective-permute-done((f32[288,384]{1,0:T(8,128)S(1)}, f32[288,384]{1,0:T(8,128)S(1)}, u32[]{:S(2)}, u32[]{:S(2)}) %collective-permute-start.1) | collective-permute-done | bytes 442400 | tf_op jit(solution)/shard_map/cond/branch_0_fun/ppermute | solution.py:574
  97.9 1.6 collective-permute-start.2
  99.5 6.8 %collective-permute-done.2 = f32[288,384]{1,0:T(8,128)S(1)} collective-permute-done((f32[288,384]{1,0:T(8,128)S(1)}, f32[288,384]{1,0:T(8,128)S(1)}, u32[]{:S(2)}, u32[]{:S(2)}) %collective-permute-start.2) | collective-permute-done | bytes 442400 | tf_op jit(solution)/shard_map/cond/branch_0_fun/ppermute | solution.py:574
  106.4 1.8 collective-permute-done.3.refs_5_
  108.2 7.2 %apply_update.3 = f32[576,384]{1,0:T(8,128)} custom-call(s32[4]{0:T(128)S(1)} %get-tuple-element.50.refs_0_, s32[4]{0:T(128)S(1)} %get-tuple-element.51.refs_1_, s32[4,4]{1,0:T(4,128)S(1)} %get-tuple-element.52.refs_2_, s32[4,4]{1,0:T(4,128)S(1)} %get-tuple-element.53.refs_3_, f32[288,384]{1,0:T(8,128)S(1)} %add.24.refs_4_, ...), custom_call_target="tpu_custom_call" | custom-call | tf_op jit(solution)/shard_map/cond/branch_0_fun/apply_update/pallas_call | solution.py:500
  119.1 1.7 collective-permute-start.23
  120.8 5.9 %fresh_momentum.1 = (f32[4,288,896]{2,1,0:T(8,128)}, f32[8,128]{1,0:T(8,128)}) custom-call(s32[4]{0:T(128)S(1)} %copy-done.8, s32[4,4]{1,0:T(4,128)S(1)} %copy-done.5, f32[4,288,896]{2,1,0:T(8,128)} %momentum.1, f32[4,288,896]{2,1,0:T(8,128)} %gradient.1, f32[8,128]{1,0:T(8,128)} %get-tuple-element.116._), custom_call_target="tpu_custom_call" | custom-call | tf_op jit(solution)/shard_map/fresh_momentum/pallas_call | solution.py:451
  127.4 7.1 %finish.1 = (f32[576,896]{1,0:T(8,128)}, f32[4,288,896]{2,1,0:T(8,128)}) custom-call(s32[4]{0:T(128)S(1)} %copy-done.7, s32[4]{0:T(128)S(1)} %copy-done.8, s32[4,4]{1,0:T(4,128)S(1)} %copy-done.5, s32[4,4]{1,0:T(4,128)S(1)} %copy-done.6, f32[576,384]{1,0:T(8,128)} %get-tuple-element.133.refs_4_, bf16[4,576,896]{2,1,0:T(8,128)(2,1)} %get-tuple-element.130.refs_5_, ...), custom_call_target="tpu_custom_call" | custom-call | tf_op jit(solution)/shard_map/finish/pallas_call | solution.py:535
  136.1 34.1 %collective-permute-done.24.refs_1_ = f32[288,896]{1,0:T(8,128)S(1)} collective-permute-done((f32[288,896]{1,0:T(8,128)}, f32[288,896]{1,0:T(8,128)S(1)}, u32[]{:S(2)}, u32[]{:S(2)}) %collective-permute-start.24) | collective-permute-done | bytes 1032224 | tf_op jit(solution)/shard_map/ppermute | solution.py:600
  171.7 19.6 %collective-permute-done.22.refs_1_ = f32[288,896]{1,0:T(8,128)} collective-permute-done((f32[288,896]{1,0:T(8,128)}, f32[288,896]{1,0:T(8,128)}, u32[]{:S(2)}, u32[]{:S(2)}) %collective-permute-start.22) | collective-permute-done | bytes 1032224 | tf_op jit(solution)/shard_map/ppermute | solution.py:600
  191.3 3.1 %place_blocks.5 = f32[4,288,896]{2,1,0:T(8,128)} custom-call(s32[4]{0:T(128)S(1)} %copy-done.7, f32[288,896]{1,0:T(8,128)} %collective-permute-done.22.refs_1_, f32[288,896]{1,0:T(8,128)} %collective-permute-done.23.refs_2_, f32[4,288,896]{2,1,0:T(8,128)} %place_blocks.4.refs_3_), custom_call_target="tpu_custom_call", output_to_operand_aliasing={{}: (3, {})} | custom-call | tf_op jit(solution)/shard_map/place_blocks/pallas_call | solution.py:557
  (48 shorter events, 16.0 us)
Async XLA Ops:
  0.6 35.6 %copy-start.7 = (s32[4]{0:T(128)S(1)}, s32[4]{0:T(128)}, u32[]{:S(2)}) copy-start(s32[4]{0:T(128)} %refs_0_.13) | copy-start | bytes 52
  0.6 35.6 %copy-start.5 = (s32[4,4]{1,0:T(4,128)S(1)}, s32[4,4]{1,0:T(4,128)}, u32[]{:S(2)}) copy-start(s32[4,4]{1,0:T(4,128)} %refs_2_.7) | copy-start | bytes 196
  0.7 35.6 %copy-start.8 = (s32[4]{0:T(128)S(1)}, s32[4]{0:T(128)}, u32[]{:S(2)}) copy-start(s32[4]{0:T(128)} %refs_1_.7) | copy-start | bytes 52
  0.7 35.5 %copy-start.6 = (s32[4,4]{1,0:T(4,128)S(1)}, s32[4,4]{1,0:T(4,128)}, u32[]{:S(2)}) copy-start(s32[4,4]{1,0:T(4,128)} %refs_3_.7) | copy-start | bytes 196
  5.5 8.5 %collective-permute-start.20 = (f32[288,896]{1,0:T(8,128)}, f32[288,896]{1,0:T(8,128)S(1)}, u32[]{:S(2)}, u32[]{:S(2)}) collective-permute-start(f32[288,896]{1,0:T(8,128)} %get-tuple-element.123), channel_id=1, source_target_pairs={{8,16},{16,8},{9,17},{17,9},{10,18},{18,10},{11,19},{19,11},{12,20... | collective-permute-start | bytes 3096584 | tf_op jit(solution)/shard_map/ppermute | solution.py:597
  6.2 29.4 %collective-permute-start.14 = (f32[288,896]{1,0:T(8,128)}, f32[288,896]{1,0:T(8,128)S(1)}, u32[]{:S(2)}, u32[]{:S(2)}) collective-permute-start(f32[288,896]{1,0:T(8,128)} %get-tuple-element.115.refs_4_), channel_id=1, source_target_pairs={{0,8},{8,0},{16,24},{24,16},{1,9},{9,1},{17,25},{25,17},{2,10},{10... | collective-permute-start | bytes 3096584 | tf_op jit(solution)/shard_map/ppermute | solution.py:606
  12.0 45.7 %collective-permute-start.18 = (f32[288,896]{1,0:T(8,128)}, f32[288,896]{1,0:T(8,128)S(1)}, u32[]{:S(2)}, u32[]{:S(2)}) collective-permute-start(f32[288,896]{1,0:T(8,128)} %get-tuple-element.122), channel_id=1, source_target_pairs={{0,16},{24,8},{1,17},{25,9},{2,18},{26,10},{3,19},{27,11},{4,20},{... | collective-permute-start | bytes 3096584 | tf_op jit(solution)/shard_map/ppermute | solution.py:597
  13.9 45.1 %collective-permute-start.21 = (f32[288,896]{1,0:T(8,128)S(1)}, f32[288,896]{1,0:T(8,128)}, u32[]{:S(2)}, u32[]{:S(2)}) collective-permute-start(f32[288,896]{1,0:T(8,128)S(1)} %collective-permute-done.20.refs_7_), channel_id=1, source_target_pairs={{8,0},{16,24},{9,1},{17,25},{10,2},{18,26},{11,3},{19,27},{12,4},{... | collective-permute-start | bytes 3096584 | tf_op jit(solution)/shard_map/ppermute | solution.py:600
  40.8 75.7 %collective-permute-start.15 = (f32[288,896]{1,0:T(8,128)}, f32[288,896]{1,0:T(8,128)}, u32[]{:S(2)}, u32[]{:S(2)}) collective-permute-start(f32[288,896]{1,0:T(8,128)} %get-tuple-element.119), channel_id=1, source_target_pairs={{0,8},{24,16},{1,9},{25,17},{2,10},{26,18},{3,11},{27,19},{4,12},{... | collective-permute-start | bytes 3096584 | tf_op jit(solution)/shard_map/ppermute | solution.py:597
  46.0 70.4 %collective-permute-start.16 = (f32[288,896]{1,0:T(8,128)}, f32[288,896]{1,0:T(8,128)}, u32[]{:S(2)}, u32[]{:S(2)}) collective-permute-start(f32[288,896]{1,0:T(8,128)} %get-tuple-element.120), channel_id=1, source_target_pairs={{0,16},{24,8},{1,17},{25,9},{2,18},{26,10},{3,19},{27,11},{4,20},{... | collective-permute-start | bytes 3096584 | tf_op jit(solution)/shard_map/ppermute | solution.py:597
  48.3 68.2 %collective-permute-start.17 = (f32[288,896]{1,0:T(8,128)}, f32[288,896]{1,0:T(8,128)}, u32[]{:S(2)}, u32[]{:S(2)}) collective-permute-start(f32[288,896]{1,0:T(8,128)} %get-tuple-element.121), channel_id=1, source_target_pairs={{8,16},{16,8},{9,17},{17,9},{10,18},{18,10},{11,19},{19,11},{12,20... | collective-permute-start | bytes 3096584 | tf_op jit(solution)/shard_map/ppermute | solution.py:597
  57.8 23.9 %collective-permute-start.19 = (f32[288,896]{1,0:T(8,128)S(1)}, f32[288,896]{1,0:T(8,128)}, u32[]{:S(2)}, u32[]{:S(2)}) collective-permute-start(f32[288,896]{1,0:T(8,128)S(1)} %collective-permute-done.18.refs_6_), channel_id=1, source_target_pairs={{8,0},{16,24},{9,1},{17,25},{10,2},{18,26},{11,3},{19,27},{12,4},{... | collective-permute-start | bytes 3096584 | tf_op jit(solution)/shard_map/ppermute | solution.py:600
  60.0 1.0 copy-start.9
  61.0 73.5 %collective-permute-start.25 = (f32[288,896]{1,0:T(8,128)}, f32[288,896]{1,0:T(8,128)S(1)}, u32[]{:S(2)}, u32[]{:S(2)}) collective-permute-start(f32[288,896]{1,0:T(8,128)} %get-tuple-element.131), channel_id=1, source_target_pairs={{8,24},{16,0},{9,25},{17,1},{10,26},{18,2},{11,27},{19,3},{12,28},... | collective-permute-start | bytes 3096584 | tf_op jit(solution)/shard_map/ppermute | solution.py:600
  81.7 34.8 %copy-start.4 = (f32[288,896]{1,0:T(8,128)S(1)}, f32[288,896]{1,0:T(8,128)}, u32[]{:S(2)}) copy-start(f32[288,896]{1,0:T(8,128)} %get-tuple-element.118) | copy-start | bytes 3096580
  87.6 27.9 %copy-start.2 = (bf16[4,576,896]{2,1,0:T(8,128)(2,1)}, bf16[4,576,896]{2,1,0:T(8,128)(2,1)S(1)}, u32[]{:S(2)}) copy-start(bf16[4,576,896]{2,1,0:T(8,128)(2,1)S(1)} %get-tuple-element.144.refs_6_) | copy-start | bytes 12386308 | tf_op jit(solution)/shard_map/cond
  87.6 1.9 collective-permute-start
  89.5 8.4 %collective-permute-start.1 = (f32[288,384]{1,0:T(8,128)S(1)}, f32[288,384]{1,0:T(8,128)S(1)}, u32[]{:S(2)}, u32[]{:S(2)}) collective-permute-start(f32[288,384]{1,0:T(8,128)S(1)} %add.22), channel_id=1, source_target_pairs={{0,2},{1,5},{2,0},{3,7},{4,6},{5,1},{6,4},{7,3},{8,10},{9,13},{10,... | collective-permute-start | bytes 1327112 | tf_op jit(solution)/shard_map/cond/branch_0_fun/ppermute | solution.py:574
  97.9 8.4 %collective-permute-start.2 = (f32[288,384]{1,0:T(8,128)S(1)}, f32[288,384]{1,0:T(8,128)S(1)}, u32[]{:S(2)}, u32[]{:S(2)}) collective-permute-start(f32[288,384]{1,0:T(8,128)S(1)} %add.23), channel_id=1, source_target_pairs={{0,4},{1,3},{2,6},{3,1},{4,0},{5,7},{6,2},{7,5},{8,12},{9,11},{10,... | collective-permute-start | bytes 1327112 | tf_op jit(solution)/shard_map/cond/branch_0_fun/ppermute | solution.py:574
  106.4 1.9 collective-permute-start.3
  115.7 18.8 %collective-permute-start.26 = (f32[288,896]{1,0:T(8,128)}, f32[288,896]{1,0:T(8,128)S(1)}, u32[]{:S(2)}, u32[]{:S(2)}) collective-permute-start(f32[288,896]{1,0:T(8,128)} %get-tuple-element.132), channel_id=1, source_target_pairs={{8,16},{16,8},{9,17},{17,9},{10,18},{18,10},{11,19},{19,11},{12,20... | collective-permute-start | bytes 3096584 | tf_op jit(solution)/shard_map/ppermute | solution.py:600
  116.5 53.7 %collective-permute-start.24 = (f32[288,896]{1,0:T(8,128)}, f32[288,896]{1,0:T(8,128)S(1)}, u32[]{:S(2)}, u32[]{:S(2)}) collective-permute-start(f32[288,896]{1,0:T(8,128)} %get-tuple-element.127), channel_id=1, source_target_pairs={{8,24},{16,0},{9,25},{17,1},{10,26},{18,2},{11,27},{19,3},{12,28},... | collective-permute-start | bytes 3096584 | tf_op jit(solution)/shard_map/ppermute | solution.py:600
  117.8 73.5 %collective-permute-start.22 = (f32[288,896]{1,0:T(8,128)}, f32[288,896]{1,0:T(8,128)}, u32[]{:S(2)}, u32[]{:S(2)}) collective-permute-start(f32[288,896]{1,0:T(8,128)} %get-tuple-element.125), channel_id=1, source_target_pairs={{8,0},{16,24},{9,1},{17,25},{10,2},{18,26},{11,3},{19,27},{12,4},{... | collective-permute-start | bytes 3096584 | tf_op jit(solution)/shard_map/ppermute | solution.py:600
  119.1 72.2 %collective-permute-start.23 = (f32[288,896]{1,0:T(8,128)}, f32[288,896]{1,0:T(8,128)}, u32[]{:S(2)}, u32[]{:S(2)}) collective-permute-start(f32[288,896]{1,0:T(8,128)} %get-tuple-element.126), channel_id=1, source_target_pairs={{8,16},{16,8},{9,17},{17,9},{10,18},{18,10},{11,19},{19,11},{12,20... | collective-permute-start | bytes 3096584 | tf_op jit(solution)/shard_map/ppermute | solution.py:600
  (2 other events, 1.3 us)

commit v3 on v0

--- a/solution.py
+++ b/solution.py
@@ -430,7 +430,7 @@
 def blend(first, tables, momentum, gradient, before):
     _, slots, columns = momentum.shape
     ranks = tables[1].shape[0]
-    chunks = 2 if slots % (2 * SUBLANES) == 0 else 1
+    chunks = 1
     return pl.pallas_call(
         functools.partial(blend_kernel, first, chunks),
         out_shape=[floats(slots, columns)] * (ranks - first) + [floats(SUBLANES, 128)],
@@ -648,7 +648,7 @@
     sources = [packed, pair, last_packed, last_pair, outer_packed, outer_pair]
     result, shards = finish(tables, sources, momentum.shape, token)
     shards = place_blocks(True, owner_group, early, first_home, shards, ranks)
-    for step, block in zip(last, last_home):
+    for step, block in sorted(zip(last, last_home), key=lambda home: (home[0] == near, last.index(home[0]))):
         shards = place_blocks(False, owner_group, [step], [block], shards, ranks)
     return (new_momentum, shards, result[None])
 

time: 194 us -> 194 us (level)
  no operation moved by 1% of the time
where the time goes in v3:
time: 194 us
  waiting for transfers between devices  117 us (60%)
  Pallas kernels  43.6 us (22%)
  starting transfers between devices  29.6 us (15%)
  local copies, waits for them, and re-layouts  2.31 us (1%)
    ppermute x7, waiting for transfers between devices, from_inner(): return lax.ppermute(block, 'fsdp', pairs(step, False))  71.5 us
    ppermute x1, waiting for transfers between devices, on_device(): swapped = lax.ppermute(own, 'fsdp', [(i, i ^ near) for i in range(ranks)])  20.4 us
    ppermute x4, waiting for transfers between devices, exchange(): lax.ppermute(piece, axis, [(i, i ^ bits[i & 1]) for i in range(size)])  17.2 us
    ppermute x5, starting transfers between devices, to_inner(): return lax.ppermute(block, 'fsdp', pairs(step, True))  11.7 us
    pallas_call x2, Pallas kernels, blend(): pl.pallas_call(functools.partial(blend_kernel, first, chunks), out_shape=...  9.83 us
    ppermute x7, starting transfers between devices, from_inner(): return lax.ppermute(block, 'fsdp', pairs(step, False))  8.81 us
    ppermute x5, waiting for transfers between devices, to_inner(): return lax.ppermute(block, 'fsdp', pairs(step, True))  7.63 us
    pallas_call x1, Pallas kernels, finish(): pl.pallas_call(functools.partial(finish_kernel, tables[1].shape[0]), out_...  7.38 us
  transfers between devices with their start and end apart: 17, of which 9 were waited for; matrix products, arithmetic and copies ran while one was open for 0% of the time, Pallas kernels for 19%

profile of v3, /device:TPU:0, one launch (start us, length us, event | category | flops | bytes accessed | tf_op | source)
XLA Modules:
  0.0 193.8 jit_solution(3249599644575347992)
XLA Ops:
  0.7 5.0 %blend.2 = (f32[288,896]{1,0:T(8,128)}, f32[288,896]{1,0:T(8,128)}, f32[288,896]{1,0:T(8,128)}, f32[8,128]{1,0:T(8,128)}) custom-call(s32[4]{0:T(128)} %refs_0_.15, s32[4]{0:T(128)} %refs_1_.7, s32[4,4]{1,0:T(4,128)} %refs_2_.7, s32[4,4]{1,0:T(4,128)} %refs_3_.7, f32[4,288,896]{2,1,0:T(8,128)} %momentum.1, f32[4,288,896]{2,1,0:T(8,128)} %gradient.1), custom_call_target="tpu_custom_call" | custom-call | tf_op jit(solution)/shard_map/blend/pallas_call | solution.py:434
  6.4 5.8 %collective-permute-start.14 = (f32[288,896]{1,0:T(8,128)}, f32[288,896]{1,0:T(8,128)S(1)}, u32[]{:S(2)}, u32[]{:S(2)}) collective-permute-start(f32[288,896]{1,0:T(8,128)} %get-tuple-element.115.refs_4_), channel_id=1, source_target_pairs={{0,8},{8,0},{16,24},{24,16},{1,9},{9,1},{17,25},{25,17},{2,10},{10... | collective-permute-start | bytes 3096584 | tf_op jit(solution)/shard_map/ppermute | solution.py:606
  12.3 1.9 collective-permute-start.18
  15.5 20.4 %collective-permute-done.14.refs_0_.refs_5_ = f32[288,896]{1,0:T(8,128)S(1)} collective-permute-done((f32[288,896]{1,0:T(8,128)}, f32[288,896]{1,0:T(8,128)S(1)}, u32[]{:S(2)}, u32[]{:S(2)}) %collective-permute-start.14) | collective-permute-done | bytes 1032224 | tf_op jit(solution)/shard_map/ppermute | solution.py:606
  36.5 4.8 %blend.3 = (f32[288,896]{1,0:T(8,128)}, f32[288,896]{1,0:T(8,128)}, f32[288,896]{1,0:T(8,128)}, f32[288,896]{1,0:T(8,128)}, f32[8,128]{1,0:T(8,128)}) custom-call(s32[4]{0:T(128)S(1)} %copy-done.7, s32[4]{0:T(128)S(1)} %copy-done.9, s32[4,4]{1,0:T(4,128)S(1)} %copy-done.5, s32[4,4]{1,0:T(4,128)S(1)} %copy-done.6, f32[4,288,896]{2,1,0:T(8,128)} %momentum.1, ...), custom_call_target="tpu_custom_call" | custom-call | tf_op jit(solution)/shard_map/blend/pallas_call | solution.py:434
  41.3 5.2 %collective-permute-start.15 = (f32[288,896]{1,0:T(8,128)}, f32[288,896]{1,0:T(8,128)}, u32[]{:S(2)}, u32[]{:S(2)}) collective-permute-start(f32[288,896]{1,0:T(8,128)} %get-tuple-element.119), channel_id=1, source_target_pairs={{0,8},{24,16},{1,9},{25,17},{2,10},{26,18},{3,11},{27,19},{4,12},{... | collective-permute-start | bytes 3096584 | tf_op jit(solution)/shard_map/ppermute | solution.py:597
  46.5 2.3 %collective-permute-start.16 = (f32[288,896]{1,0:T(8,128)}, f32[288,896]{1,0:T(8,128)}, u32[]{:S(2)}, u32[]{:S(2)}) collective-permute-start(f32[288,896]{1,0:T(8,128)} %get-tuple-element.120), channel_id=1, source_target_pairs={{0,16},{24,8},{1,17},{25,9},{2,18},{26,10},{3,19},{27,11},{4,20},{... | collective-permute-start | bytes 3096584 | tf_op jit(solution)/shard_map/ppermute | solution.py:597
  48.8 1.6 collective-permute-start.17
  50.4 7.6 %collective-permute-done.18.refs_6_ = f32[288,896]{1,0:T(8,128)S(1)} collective-permute-done((f32[288,896]{1,0:T(8,128)}, f32[288,896]{1,0:T(8,128)S(1)}, u32[]{:S(2)}, u32[]{:S(2)}) %collective-permute-start.18) | collective-permute-done | bytes 1032224 | tf_op jit(solution)/shard_map/ppermute | solution.py:597
  62.5 19.4 %collective-permute-done.19 = f32[288,896]{1,0:T(8,128)} collective-permute-done((f32[288,896]{1,0:T(8,128)S(1)}, f32[288,896]{1,0:T(8,128)}, u32[]{:S(2)}, u32[]{:S(2)}) %collective-permute-start.19) | collective-permute-done | bytes 1032224 | tf_op jit(solution)/shard_map/ppermute | solution.py:600
  81.9 34.1 %conditional.3 = ((bf16[4,576,896]{2,1,0:T(8,128)(2,1)}, f32[576,384]{1,0:T(8,128)})) conditional(s32[]{:T(128)} %convert_element_type.2, (s32[4]{0:T(128)S(1)}, s32[4]{0:T(128)S(1)}, s32[4,4]{1,0:T(4,128)S(1)}, s32[4,4]{1,0:T(4,128)S(1)}, f32[288,896]{1,0:T(8,128)S(1)}, /*index=5*/f32[288,896]{1,0:T(8,128)}, f32[288,896]{1,0:T(8,128)}, ...), branch_computations={%region_0.0_spmd, %region_1.0_spmd} | conditional | flops 331776 | bytes 27574484 | solution.py:636
  81.9 5.9 %assemble_and_gram.3 = (bf16[4,576,896]{2,1,0:T(8,128)(2,1)S(1)}, f32[288,384]{1,0:T(8,128)S(1)}, f32[288,384]{1,0:T(8,128)S(1)}) custom-call(s32[4]{0:T(128)S(1)} %get-tuple-element.50.refs_0_, s32[4]{0:T(128)S(1)} %get-tuple-element.51.refs_1_, s32[4,4]{1,0:T(4,128)S(1)} %get-tuple-element.52.refs_2_, s32[4,4]{1,0:T(4,128)S(1)} %get-tuple-element.53.refs_3_, ...), custom_call_target="tpu_custom_call" | custom-call | tf_op jit(solution)/shard_map/cond/branch_0_fun/assemble_and_gram/pallas_call | solution.py:467
  87.9 1.8 collective-permute-done
  91.3 6.8 %collective-permute-done.1 = f32[288,384]{1,0:T(8,128)S(1)} collective-permute-done((f32[288,384]{1,0:T(8,128)S(1)}, f32[288,384]{1,0:T(8,128)S(1)}, u32[]{:S(2)}, u32[]{:S(2)}) %collective-permute-start.1) | collective-permute-done | bytes 442400 | tf_op jit(solution)/shard_map/cond/branch_0_fun/ppermute | solution.py:574
  98.2 1.6 collective-permute-start.2
  99.8 6.8 %collective-permute-done.2 = f32[288,384]{1,0:T(8,128)S(1)} collective-permute-done((f32[288,384]{1,0:T(8,128)S(1)}, f32[288,384]{1,0:T(8,128)S(1)}, u32[]{:S(2)}, u32[]{:S(2)}) %collective-permute-start.2) | collective-permute-done | bytes 442400 | tf_op jit(solution)/shard_map/cond/branch_0_fun/ppermute | solution.py:574
  106.7 1.8 collective-permute-done.3.refs_5_
  108.5 7.3 %apply_update.3 = f32[576,384]{1,0:T(8,128)} custom-call(s32[4]{0:T(128)S(1)} %get-tuple-element.50.refs_0_, s32[4]{0:T(128)S(1)} %get-tuple-element.51.refs_1_, s32[4,4]{1,0:T(4,128)S(1)} %get-tuple-element.52.refs_2_, s32[4,4]{1,0:T(4,128)S(1)} %get-tuple-element.53.refs_3_, f32[288,384]{1,0:T(8,128)S(1)} %add.24.refs_4_, ...), custom_call_target="tpu_custom_call" | custom-call | tf_op jit(solution)/shard_map/cond/branch_0_fun/apply_update/pallas_call | solution.py:500
  116.0 1.6 collective-permute-start.26
  121.0 5.9 %fresh_momentum.1 = (f32[4,288,896]{2,1,0:T(8,128)}, f32[8,128]{1,0:T(8,128)}) custom-call(s32[4]{0:T(128)} %refs_1_.7, s32[4,4]{1,0:T(4,128)} %refs_2_.7, f32[4,288,896]{2,1,0:T(8,128)} %momentum.1, f32[4,288,896]{2,1,0:T(8,128)} %gradient.1, f32[8,128]{1,0:T(8,128)} %get-tuple-element.116._), custom_call_target="tpu_custom_call" | custom-call | tf_op jit(solution)/shard_map/fresh_momentum/pallas_call | solution.py:451
  127.6 7.4 %finish.1 = (f32[576,896]{1,0:T(8,128)}, f32[4,288,896]{2,1,0:T(8,128)}) custom-call(s32[4]{0:T(128)} %refs_0_.15, s32[4]{0:T(128)} %refs_1_.7, s32[4,4]{1,0:T(4,128)} %refs_2_.7, s32[4,4]{1,0:T(4,128)} %refs_3_.7, f32[576,384]{1,0:T(8,128)} %get-tuple-element.133.refs_4_, bf16[4,576,896]{2,1,0:T(8,128)(2,1)} %get-tuple-element.130.refs_5_, ...), custom_call_target="tpu_custom_call" | custom-call | tf_op jit(solution)/shard_map/finish/pallas_call | solution.py:535
  135.1 2.8 %place_blocks.4.refs_2_ = f32[4,288,896]{2,1,0:T(8,128)} custom-call(s32[4]{0:T(128)S(1)} %copy-done.8, f32[288,896]{1,0:T(8,128)S(1)} %collective-permute-done.25.refs_1_, f32[288,896]{1,0:T(8,128)} %collective-permute-done.26.refs_2_, f32[4,288,896]{2,1,0:T(8,128)} %get-tuple-element.138.refs_3_), custom_call_target="tpu_custom_call", output_to_operand_aliasing={{}: (3, {})} | custom-call | tf_op jit(solution)/shard_map/place_blocks/pallas_call | solution.py:557
  137.8 32.7 %collective-permute-done.24.refs_1_ = f32[288,896]{1,0:T(8,128)S(1)} collective-permute-done((f32[288,896]{1,0:T(8,128)}, f32[288,896]{1,0:T(8,128)S(1)}, u32[]{:S(2)}, u32[]{:S(2)}) %collective-permute-start.24) | collective-permute-done | bytes 1032224 | tf_op jit(solution)/shard_map/ppermute | solution.py:600
  172.6 19.5 %collective-permute-done.22.refs_1_ = f32[288,896]{1,0:T(8,128)S(1)} collective-permute-done((f32[288,896]{1,0:T(8,128)}, f32[288,896]{1,0:T(8,128)S(1)}, u32[]{:S(2)}, u32[]{:S(2)}) %collective-permute-start.22) | collective-permute-done | bytes 1032224 | tf_op jit(solution)/shard_map/ppermute | solution.py:600
  (51 shorter events, 16.6 us)
Async XLA Ops:
  0.6 35.8 %copy-start.7 = (s32[4]{0:T(128)S(1)}, s32[4]{0:T(128)}, u32[]{:S(2)}) copy-start(s32[4]{0:T(128)} %refs_0_.15) | copy-start | bytes 52
  0.6 35.8 %copy-start.5 = (s32[4,4]{1,0:T(4,128)S(1)}, s32[4,4]{1,0:T(4,128)}, u32[]{:S(2)}) copy-start(s32[4,4]{1,0:T(4,128)} %refs_2_.7) | copy-start | bytes 196
  0.7 35.8 %copy-start.9 = (s32[4]{0:T(128)S(1)}, s32[4]{0:T(128)}, u32[]{:S(2)}) copy-start(s32[4]{0:T(128)} %refs_1_.7) | copy-start | bytes 52
  0.7 35.8 %copy-start.6 = (s32[4,4]{1,0:T(4,128)S(1)}, s32[4,4]{1,0:T(4,128)}, u32[]{:S(2)}) copy-start(s32[4,4]{1,0:T(4,128)} %refs_3_.7) | copy-start | bytes 196
  5.7 8.5 %collective-permute-start.20 = (f32[288,896]{1,0:T(8,128)}, f32[288,896]{1,0:T(8,128)S(1)}, u32[]{:S(2)}, u32[]{:S(2)}) collective-permute-start(f32[288,896]{1,0:T(8,128)} %get-tuple-element.123), channel_id=1, source_target_pairs={{8,16},{16,8},{9,17},{17,9},{10,18},{18,10},{11,19},{19,11},{12,20... | collective-permute-start | bytes 3096584 | tf_op jit(solution)/shard_map/ppermute | solution.py:597
  6.4 29.4 %collective-permute-start.14 = (f32[288,896]{1,0:T(8,128)}, f32[288,896]{1,0:T(8,128)S(1)}, u32[]{:S(2)}, u32[]{:S(2)}) collective-permute-start(f32[288,896]{1,0:T(8,128)} %get-tuple-element.115.refs_4_), channel_id=1, source_target_pairs={{0,8},{8,0},{16,24},{24,16},{1,9},{9,1},{17,25},{25,17},{2,10},{10... | collective-permute-start | bytes 3096584 | tf_op jit(solution)/shard_map/ppermute | solution.py:606
  12.3 45.7 %collective-permute-start.18 = (f32[288,896]{1,0:T(8,128)}, f32[288,896]{1,0:T(8,128)S(1)}, u32[]{:S(2)}, u32[]{:S(2)}) collective-permute-start(f32[288,896]{1,0:T(8,128)} %get-tuple-element.122), channel_id=1, source_target_pairs={{0,16},{24,8},{1,17},{25,9},{2,18},{26,10},{3,19},{27,11},{4,20},{... | collective-permute-start | bytes 3096584 | tf_op jit(solution)/shard_map/ppermute | solution.py:597
  14.2 45.1 %collective-permute-start.21 = (f32[288,896]{1,0:T(8,128)S(1)}, f32[288,896]{1,0:T(8,128)}, u32[]{:S(2)}, u32[]{:S(2)}) collective-permute-start(f32[288,896]{1,0:T(8,128)S(1)} %collective-permute-done.20.refs_7_), channel_id=1, source_target_pairs={{8,0},{16,24},{9,1},{17,25},{10,2},{18,26},{11,3},{19,27},{12,4},{... | collective-permute-start | bytes 3096584 | tf_op jit(solution)/shard_map/ppermute | solution.py:600
  41.3 76.4 %collective-permute-start.15 = (f32[288,896]{1,0:T(8,128)}, f32[288,896]{1,0:T(8,128)}, u32[]{:S(2)}, u32[]{:S(2)}) collective-permute-start(f32[288,896]{1,0:T(8,128)} %get-tuple-element.119), channel_id=1, source_target_pairs={{0,8},{24,16},{1,9},{25,17},{2,10},{26,18},{3,11},{27,19},{4,12},{... | collective-permute-start | bytes 3096584 | tf_op jit(solution)/shard_map/ppermute | solution.py:597
  46.5 71.1 %collective-permute-start.16 = (f32[288,896]{1,0:T(8,128)}, f32[288,896]{1,0:T(8,128)}, u32[]{:S(2)}, u32[]{:S(2)}) collective-permute-start(f32[288,896]{1,0:T(8,128)} %get-tuple-element.120), channel_id=1, source_target_pairs={{0,16},{24,8},{1,17},{25,9},{2,18},{26,10},{3,19},{27,11},{4,20},{... | collective-permute-start | bytes 3096584 | tf_op jit(solution)/shard_map/ppermute | solution.py:597
  48.8 68.9 %collective-permute-start.17 = (f32[288,896]{1,0:T(8,128)}, f32[288,896]{1,0:T(8,128)}, u32[]{:S(2)}, u32[]{:S(2)}) collective-permute-start(f32[288,896]{1,0:T(8,128)} %get-tuple-element.121), channel_id=1, source_target_pairs={{8,16},{16,8},{9,17},{17,9},{10,18},{18,10},{11,19},{19,11},{12,20... | collective-permute-start | bytes 3096584 | tf_op jit(solution)/shard_map/ppermute | solution.py:597
  58.0 23.9 %collective-permute-start.19 = (f32[288,896]{1,0:T(8,128)S(1)}, f32[288,896]{1,0:T(8,128)}, u32[]{:S(2)}, u32[]{:S(2)}) collective-permute-start(f32[288,896]{1,0:T(8,128)S(1)} %collective-permute-done.18.refs_6_), channel_id=1, source_target_pairs={{8,0},{16,24},{9,1},{17,25},{10,2},{18,26},{11,3},{19,27},{12,4},{... | collective-permute-start | bytes 3096584 | tf_op jit(solution)/shard_map/ppermute | solution.py:600
  61.2 73.8 %collective-permute-start.25 = (f32[288,896]{1,0:T(8,128)}, f32[288,896]{1,0:T(8,128)S(1)}, u32[]{:S(2)}, u32[]{:S(2)}) collective-permute-start(f32[288,896]{1,0:T(8,128)} %get-tuple-element.131), channel_id=1, source_target_pairs={{8,24},{16,0},{9,25},{17,1},{10,26},{18,2},{11,27},{19,3},{12,28},... | collective-permute-start | bytes 3096584 | tf_op jit(solution)/shard_map/ppermute | solution.py:600
  81.9 35.7 %copy-start.4 = (f32[288,896]{1,0:T(8,128)S(1)}, f32[288,896]{1,0:T(8,128)}, u32[]{:S(2)}) copy-start(f32[288,896]{1,0:T(8,128)} %get-tuple-element.118) | copy-start | bytes 3096580
  87.9 27.9 %copy-start.2 = (bf16[4,576,896]{2,1,0:T(8,128)(2,1)}, bf16[4,576,896]{2,1,0:T(8,128)(2,1)S(1)}, u32[]{:S(2)}) copy-start(bf16[4,576,896]{2,1,0:T(8,128)(2,1)S(1)} %get-tuple-element.144.refs_6_) | copy-start | bytes 12386308 | tf_op jit(solution)/shard_map/cond
  87.9 1.9 collective-permute-start
  89.8 8.4 %collective-permute-start.1 = (f32[288,384]{1,0:T(8,128)S(1)}, f32[288,384]{1,0:T(8,128)S(1)}, u32[]{:S(2)}, u32[]{:S(2)}) collective-permute-start(f32[288,384]{1,0:T(8,128)S(1)} %add.22), channel_id=1, source_target_pairs={{0,2},{1,5},{2,0},{3,7},{4,6},{5,1},{6,4},{7,3},{8,10},{9,13},{10,... | collective-permute-start | bytes 1327112 | tf_op jit(solution)/shard_map/cond/branch_0_fun/ppermute | solution.py:574
  98.2 8.4 %collective-permute-start.2 = (f32[288,384]{1,0:T(8,128)S(1)}, f32[288,384]{1,0:T(8,128)S(1)}, u32[]{:S(2)}, u32[]{:S(2)}) collective-permute-start(f32[288,384]{1,0:T(8,128)S(1)} %add.23), channel_id=1, source_target_pairs={{0,4},{1,3},{2,6},{3,1},{4,0},{5,7},{6,2},{7,5},{8,12},{9,11},{10,... | collective-permute-start | bytes 1327112 | tf_op jit(solution)/shard_map/cond/branch_0_fun/ppermute | solution.py:574
  106.6 1.9 collective-permute-start.3
  116.0 19.1 %collective-permute-start.26 = (f32[288,896]{1,0:T(8,128)}, f32[288,896]{1,0:T(8,128)}, u32[]{:S(2)}, u32[]{:S(2)}) collective-permute-start(f32[288,896]{1,0:T(8,128)} %get-tuple-element.132), channel_id=1, source_target_pairs={{8,16},{16,8},{9,17},{17,9},{10,18},{18,10},{11,19},{19,11},{12,20... | collective-permute-start | bytes 3096584 | tf_op jit(solution)/shard_map/ppermute | solution.py:600
  117.7 52.8 %collective-permute-start.24 = (f32[288,896]{1,0:T(8,128)}, f32[288,896]{1,0:T(8,128)S(1)}, u32[]{:S(2)}, u32[]{:S(2)}) collective-permute-start(f32[288,896]{1,0:T(8,128)} %get-tuple-element.127), channel_id=1, source_target_pairs={{8,24},{16,0},{9,25},{17,1},{10,26},{18,2},{11,27},{19,3},{12,28},... | collective-permute-start | bytes 3096584 | tf_op jit(solution)/shard_map/ppermute | solution.py:600
  119.0 53.0 %collective-permute-start.23 = (f32[288,896]{1,0:T(8,128)}, f32[288,896]{1,0:T(8,128)S(1)}, u32[]{:S(2)}, u32[]{:S(2)}) collective-permute-start(f32[288,896]{1,0:T(8,128)} %get-tuple-element.126), channel_id=1, source_target_pairs={{8,16},{16,8},{9,17},{17,9},{10,18},{18,10},{11,19},{19,11},{12,20... | collective-permute-start | bytes 3096584 | tf_op jit(solution)/shard_map/ppermute | solution.py:600
  119.7 72.3 %collective-permute-start.22 = (f32[288,896]{1,0:T(8,128)}, f32[288,896]{1,0:T(8,128)S(1)}, u32[]{:S(2)}, u32[]{:S(2)}) collective-permute-start(f32[288,896]{1,0:T(8,128)} %get-tuple-element.125), channel_id=1, source_target_pairs={{8,0},{16,24},{9,1},{17,25},{10,2},{18,26},{11,3},{19,27},{12,4},{... | collective-permute-start | bytes 3096584 | tf_op jit(solution)/shard_map/ppermute | solution.py:600
  127.6 7.4 %copy-start.8 = (s32[4]{0:T(128)S(1)}, s32[4]{0:T(128)}, u32[]{:S(2)}) copy-start(s32[4]{0:T(128)} %refs_0_.15) | copy-start | bytes 52
  (3 other events, 2.3 us)

commit v4 on v3

--- a/solution.py
+++ b/solution.py
@@ -192,11 +192,15 @@
     for step in range(ranks):
         copies.append(pltpu.make_async_copy(blocks[step], landed.at[step], arrive.at[step]))
         copies[-1].start()
-    owner_group, _, _, row_offsets = fetch_tables(tables, held)
+    table_copies, (owner_group, _, _, row_offsets) = table_jobs(tables, held)
+    for copy in table_copies:
+        copy.start()
+    padded[...] = jnp.zeros_like(padded)
+    for copy in table_copies:
+        copy.wait()
     rank = lax.axis_index("fsdp")
     base = jnp.where(is_inner(rank, ranks), rank, rank ^ mate(ranks))
     matrix = matrix_of(owner_group, base ^ mate(ranks) if first else base)
-    padded[...] = jnp.zeros_like(padded)
     sublane = lax.broadcasted_iota(jnp.int32, (SUBLANES, columns), 0)
     for step in range(ranks):
         start = row_offsets[matrix, base ^ step]
@@ -430,7 +434,7 @@
 def blend(first, tables, momentum, gradient, before):
     _, slots, columns = momentum.shape
     ranks = tables[1].shape[0]
-    chunks = 1
+    chunks = 2 if slots % (2 * SUBLANES) == 0 else 1
     return pl.pallas_call(
         functools.partial(blend_kernel, first, chunks),
         out_shape=[floats(slots, columns)] * (ranks - first) + [floats(SUBLANES, 128)],
@@ -518,16 +522,16 @@
     )(*tables, keep, away, pair, *after)
 
 
-def touch(value, flops=0):
+def touch(*values, flops=0):
     return pl.pallas_call(
         idle_kernel,
         out_shape=floats(SUBLANES, 128),
-        in_specs=[ANY],
+        in_specs=[ANY] * len(values),
         out_specs=ANY,
         compiler_params=SMALL,
         cost_estimate=pl.CostEstimate(flops=flops, bytes_accessed=0, transcendentals=0),
         name="touch",
-    )(value)
+    )(*values)
 
 
 def finish(tables, sources, shape, after):
@@ -622,7 +626,7 @@
     def first_skip(*_):
         return nothing(update_shapes(early, slots, columns))
 
-    packed, *homes = lax.cond(inner, first_update, first_skip, pair, keep, send, touch(keep, 10**11))
+    packed, *homes = lax.cond(inner, first_update, first_skip, pair, keep, send, touch(keep, send, flops=10**11))
     first_home = [from_inner(block, step) for step, block in zip(early, homes)]
     pair_shape = jax.ShapeDtypeStruct(pair.shape, pair.dtype)
 

time: 194 us -> 193 us (level)
  no operation moved by 1% of the time
where the time goes in v4:
time: 193 us; the launch traced here: 192 us
  waiting for transfers between devices  118 us (61%)
  Pallas kernels  42.3 us (22%)
  starting transfers between devices  29.7 us (15%)
    ppermute x7, waiting for transfers between devices, from_inner(): return lax.ppermute(block, 'fsdp', pairs(step, False))  72.2 us
    ppermute x1, waiting for transfers between devices, on_device(): swapped = lax.ppermute(own, 'fsdp', [(i, i ^ near) for i in range(ranks)])  20.4 us
    ppermute x4, waiting for transfers between devices, exchange(): lax.ppermute(piece, axis, [(i, i ^ bits[i & 1]) for i in range(size)])  17.2 us
    ppermute x5, starting transfers between devices, to_inner(): return lax.ppermute(block, 'fsdp', pairs(step, True))  11.8 us
    pallas_call x2, Pallas kernels, blend(): pl.pallas_call(functools.partial(blend_kernel, first, chunks), out_shape=...  9.33 us
    ppermute x7, starting transfers between devices, from_inner(): return lax.ppermute(block, 'fsdp', pairs(step, False))  8.81 us
    ppermute x5, waiting for transfers between devices, to_inner(): return lax.ppermute(block, 'fsdp', pairs(step, True))  7.85 us
    pallas_call x1, Pallas kernels, finish(): pl.pallas_call(functools.partial(finish_kernel, tables[1].shape[0]), out_...  7.38 us
  transfers between devices with their start and end apart: 17, of which 9 were waited for; matrix products, arithmetic and copies ran while one was open for 0% of the time, Pallas kernels for 19%

profile of v4, /device:TPU:0, one launch (start us, length us, event | category | flops | bytes accessed | tf_op | source)
XLA Modules:
  0.0 192.4 jit_solution(13029957654069823305)
XLA Ops:
  0.7 4.8 %blend.2 = (f32[288,896]{1,0:T(8,128)}, f32[288,896]{1,0:T(8,128)}, f32[288,896]{1,0:T(8,128)}, f32[8,128]{1,0:T(8,128)}) custom-call(s32[4]{0:T(128)} %refs_0_.15, s32[4]{0:T(128)} %refs_1_.7, s32[4,4]{1,0:T(4,128)} %refs_2_.7, s32[4,4]{1,0:T(4,128)} %refs_3_.7, f32[4,288,896]{2,1,0:T(8,128)} %momentum.1, f32[4,288,896]{2,1,0:T(8,128)} %gradient.1), custom_call_target="tpu_custom_call" | custom-call | tf_op jit(solution)/shard_map/blend/pallas_call | solution.py:438
  6.2 5.8 %collective-permute-start.14 = (f32[288,896]{1,0:T(8,128)}, f32[288,896]{1,0:T(8,128)S(1)}, u32[]{:S(2)}, u32[]{:S(2)}) collective-permute-start(f32[288,896]{1,0:T(8,128)} %get-tuple-element.115.refs_4_), channel_id=1, source_target_pairs={{0,8},{8,0},{16,24},{24,16},{1,9},{9,1},{17,25},{25,17},{2,10},{10... | collective-permute-start | bytes 3096584 | tf_op jit(solution)/shard_map/ppermute | solution.py:610
  12.1 1.9 collective-permute-start.18
  15.3 20.4 %collective-permute-done.14.refs_0_.refs_5_ = f32[288,896]{1,0:T(8,128)S(1)} collective-permute-done((f32[288,896]{1,0:T(8,128)}, f32[288,896]{1,0:T(8,128)S(1)}, u32[]{:S(2)}, u32[]{:S(2)}) %collective-permute-start.14) | collective-permute-done | bytes 1032224 | tf_op jit(solution)/shard_map/ppermute | solution.py:610
  36.2 4.5 %blend.3 = (f32[288,896]{1,0:T(8,128)}, f32[288,896]{1,0:T(8,128)}, f32[288,896]{1,0:T(8,128)}, f32[288,896]{1,0:T(8,128)}, f32[8,128]{1,0:T(8,128)}) custom-call(s32[4]{0:T(128)S(1)} %copy-done.7, s32[4]{0:T(128)S(1)} %copy-done.9, s32[4,4]{1,0:T(4,128)S(1)} %copy-done.5, s32[4,4]{1,0:T(4,128)S(1)} %copy-done.6, f32[4,288,896]{2,1,0:T(8,128)} %momentum.1, ...), custom_call_target="tpu_custom_call" | custom-call | tf_op jit(solution)/shard_map/blend/pallas_call | solution.py:438
  40.8 5.3 %collective-permute-start.15 = (f32[288,896]{1,0:T(8,128)}, f32[288,896]{1,0:T(8,128)}, u32[]{:S(2)}, u32[]{:S(2)}) collective-permute-start(f32[288,896]{1,0:T(8,128)} %get-tuple-element.119), channel_id=1, source_target_pairs={{0,8},{24,16},{1,9},{25,17},{2,10},{26,18},{3,11},{27,19},{4,12},{... | collective-permute-start | bytes 3096584 | tf_op jit(solution)/shard_map/ppermute | solution.py:601
  46.0 2.3 %collective-permute-start.16 = (f32[288,896]{1,0:T(8,128)}, f32[288,896]{1,0:T(8,128)}, u32[]{:S(2)}, u32[]{:S(2)}) collective-permute-start(f32[288,896]{1,0:T(8,128)} %get-tuple-element.120), channel_id=1, source_target_pairs={{0,16},{24,8},{1,17},{25,9},{2,18},{26,10},{3,19},{27,11},{4,20},{... | collective-permute-start | bytes 3096584 | tf_op jit(solution)/shard_map/ppermute | solution.py:601
  48.3 1.6 collective-permute-start.17
  49.9 7.8 %collective-permute-done.18.refs_6_ = f32[288,896]{1,0:T(8,128)S(1)} collective-permute-done((f32[288,896]{1,0:T(8,128)}, f32[288,896]{1,0:T(8,128)S(1)}, u32[]{:S(2)}, u32[]{:S(2)}) %collective-permute-start.18) | collective-permute-done | bytes 1032224 | tf_op jit(solution)/shard_map/ppermute | solution.py:601
  60.5 21.1 %collective-permute-done.19 = f32[288,896]{1,0:T(8,128)} collective-permute-done((f32[288,896]{1,0:T(8,128)S(1)}, f32[288,896]{1,0:T(8,128)}, u32[]{:S(2)}, u32[]{:S(2)}) %collective-permute-start.19) | collective-permute-done | bytes 1032224 | tf_op jit(solution)/shard_map/ppermute | solution.py:604
  81.7 34.1 %conditional.3 = ((bf16[4,576,896]{2,1,0:T(8,128)(2,1)}, f32[576,384]{1,0:T(8,128)})) conditional(s32[]{:T(128)} %convert_element_type.2, (s32[4]{0:T(128)S(1)}, s32[4]{0:T(128)S(1)}, s32[4,4]{1,0:T(4,128)S(1)}, s32[4,4]{1,0:T(4,128)S(1)}, f32[288,896]{1,0:T(8,128)S(1)}, /*index=5*/f32[288,896]{1,0:T(8,128)}, f32[288,896]{1,0:T(8,128)}, ...), branch_computations={%region_0.0_spmd, %region_1.0_spmd} | conditional | flops 331776 | bytes 27574484 | solution.py:640
  81.7 5.9 %assemble_and_gram.3 = (bf16[4,576,896]{2,1,0:T(8,128)(2,1)S(1)}, f32[288,384]{1,0:T(8,128)S(1)}, f32[288,384]{1,0:T(8,128)S(1)}) custom-call(s32[4]{0:T(128)S(1)} %get-tuple-element.50.refs_0_, s32[4]{0:T(128)S(1)} %get-tuple-element.51.refs_1_, s32[4,4]{1,0:T(4,128)S(1)} %get-tuple-element.52.refs_2_, s32[4,4]{1,0:T(4,128)S(1)} %get-tuple-element.53.refs_3_, ...), custom_call_target="tpu_custom_call" | custom-call | tf_op jit(solution)/shard_map/cond/branch_0_fun/assemble_and_gram/pallas_call | solution.py:471
  87.7 1.8 collective-permute-done
  91.1 6.8 %collective-permute-done.1 = f32[288,384]{1,0:T(8,128)S(1)} collective-permute-done((f32[288,384]{1,0:T(8,128)S(1)}, f32[288,384]{1,0:T(8,128)S(1)}, u32[]{:S(2)}, u32[]{:S(2)}) %collective-permute-start.1) | collective-permute-done | bytes 442400 | tf_op jit(solution)/shard_map/cond/branch_0_fun/ppermute | solution.py:578
  98.0 1.6 collective-permute-start.2
  99.5 6.8 %collective-permute-done.2 = f32[288,384]{1,0:T(8,128)S(1)} collective-permute-done((f32[288,384]{1,0:T(8,128)S(1)}, f32[288,384]{1,0:T(8,128)S(1)}, u32[]{:S(2)}, u32[]{:S(2)}) %collective-permute-start.2) | collective-permute-done | bytes 442400 | tf_op jit(solution)/shard_map/cond/branch_0_fun/ppermute | solution.py:578
  106.5 1.8 collective-permute-done.3.refs_5_
  108.2 7.3 %apply_update.3 = f32[576,384]{1,0:T(8,128)} custom-call(s32[4]{0:T(128)S(1)} %get-tuple-element.50.refs_0_, s32[4]{0:T(128)S(1)} %get-tuple-element.51.refs_1_, s32[4,4]{1,0:T(4,128)S(1)} %get-tuple-element.52.refs_2_, s32[4,4]{1,0:T(4,128)S(1)} %get-tuple-element.53.refs_3_, f32[288,384]{1,0:T(8,128)S(1)} %add.24.refs_4_, ...), custom_call_target="tpu_custom_call" | custom-call | tf_op jit(solution)/shard_map/cond/branch_0_fun/apply_update/pallas_call | solution.py:504
  115.7 1.6 collective-permute-start.26
  120.8 5.9 %fresh_momentum.1 = (f32[4,288,896]{2,1,0:T(8,128)}, f32[8,128]{1,0:T(8,128)}) custom-call(s32[4]{0:T(128)} %refs_1_.7, s32[4,4]{1,0:T(4,128)} %refs_2_.7, f32[4,288,896]{2,1,0:T(8,128)} %momentum.1, f32[4,288,896]{2,1,0:T(8,128)} %gradient.1, f32[8,128]{1,0:T(8,128)} %get-tuple-element.116._), custom_call_target="tpu_custom_call" | custom-call | tf_op jit(solution)/shard_map/fresh_momentum/pallas_call | solution.py:455
  127.4 7.4 %finish.1 = (f32[576,896]{1,0:T(8,128)}, f32[4,288,896]{2,1,0:T(8,128)}) custom-call(s32[4]{0:T(128)} %refs_0_.15, s32[4]{0:T(128)} %refs_1_.7, s32[4,4]{1,0:T(4,128)} %refs_2_.7, s32[4,4]{1,0:T(4,128)} %refs_3_.7, f32[576,384]{1,0:T(8,128)} %get-tuple-element.133.refs_4_, bf16[4,576,896]{2,1,0:T(8,128)(2,1)} %get-tuple-element.130.refs_5_, ...), custom_call_target="tpu_custom_call" | custom-call | tf_op jit(solution)/shard_map/finish/pallas_call | solution.py:539
  134.8 2.8 %place_blocks.4.refs_2_ = f32[4,288,896]{2,1,0:T(8,128)} custom-call(s32[4]{0:T(128)S(1)} %copy-done.8, f32[288,896]{1,0:T(8,128)S(1)} %collective-permute-done.25.refs_1_, f32[288,896]{1,0:T(8,128)} %collective-permute-done.26.refs_2_, f32[4,288,896]{2,1,0:T(8,128)} %get-tuple-element.138.refs_3_), custom_call_target="tpu_custom_call", output_to_operand_aliasing={{}: (3, {})} | custom-call | tf_op jit(solution)/shard_map/place_blocks/pallas_call | solution.py:561
  137.6 31.2 %collective-permute-done.24.refs_1_ = f32[288,896]{1,0:T(8,128)S(1)} collective-permute-done((f32[288,896]{1,0:T(8,128)}, f32[288,896]{1,0:T(8,128)S(1)}, u32[]{:S(2)}, u32[]{:S(2)}) %collective-permute-start.24) | collective-permute-done | bytes 1032224 | tf_op jit(solution)/shard_map/ppermute | solution.py:604
  170.8 19.9 %collective-permute-done.22.refs_1_ = f32[288,896]{1,0:T(8,128)S(1)} collective-permute-done((f32[288,896]{1,0:T(8,128)}, f32[288,896]{1,0:T(8,128)S(1)}, u32[]{:S(2)}, u32[]{:S(2)}) %collective-permute-start.22) | collective-permute-done | bytes 1032224 | tf_op jit(solution)/shard_map/ppermute | solution.py:604
  (49 shorter events, 14.8 us)
Async XLA Ops:
  0.6 35.6 %copy-start.7 = (s32[4]{0:T(128)S(1)}, s32[4]{0:T(128)}, u32[]{:S(2)}) copy-start(s32[4]{0:T(128)} %refs_0_.15) | copy-start | bytes 52
  0.6 35.6 %copy-start.5 = (s32[4,4]{1,0:T(4,128)S(1)}, s32[4,4]{1,0:T(4,128)}, u32[]{:S(2)}) copy-start(s32[4,4]{1,0:T(4,128)} %refs_2_.7) | copy-start | bytes 196
  0.7 35.6 %copy-start.9 = (s32[4]{0:T(128)S(1)}, s32[4]{0:T(128)}, u32[]{:S(2)}) copy-start(s32[4]{0:T(128)} %refs_1_.7) | copy-start | bytes 52
  0.7 35.6 %copy-start.6 = (s32[4,4]{1,0:T(4,128)S(1)}, s32[4,4]{1,0:T(4,128)}, u32[]{:S(2)}) copy-start(s32[4,4]{1,0:T(4,128)} %refs_3_.7) | copy-start | bytes 196
  5.5 8.5 %collective-permute-start.20 = (f32[288,896]{1,0:T(8,128)}, f32[288,896]{1,0:T(8,128)S(1)}, u32[]{:S(2)}, u32[]{:S(2)}) collective-permute-start(f32[288,896]{1,0:T(8,128)} %get-tuple-element.123), channel_id=1, source_target_pairs={{8,16},{16,8},{9,17},{17,9},{10,18},{18,10},{11,19},{19,11},{12,20... | collective-permute-start | bytes 3096584 | tf_op jit(solution)/shard_map/ppermute | solution.py:601
  6.2 29.4 %collective-permute-start.14 = (f32[288,896]{1,0:T(8,128)}, f32[288,896]{1,0:T(8,128)S(1)}, u32[]{:S(2)}, u32[]{:S(2)}) collective-permute-start(f32[288,896]{1,0:T(8,128)} %get-tuple-element.115.refs_4_), channel_id=1, source_target_pairs={{0,8},{8,0},{16,24},{24,16},{1,9},{9,1},{17,25},{25,17},{2,10},{10... | collective-permute-start | bytes 3096584 | tf_op jit(solution)/shard_map/ppermute | solution.py:610
  12.1 45.7 %collective-permute-start.18 = (f32[288,896]{1,0:T(8,128)}, f32[288,896]{1,0:T(8,128)S(1)}, u32[]{:S(2)}, u32[]{:S(2)}) collective-permute-start(f32[288,896]{1,0:T(8,128)} %get-tuple-element.122), channel_id=1, source_target_pairs={{0,16},{24,8},{1,17},{25,9},{2,18},{26,10},{3,19},{27,11},{4,20},{... | collective-permute-start | bytes 3096584 | tf_op jit(solution)/shard_map/ppermute | solution.py:601
  13.9 45.1 %collective-permute-start.21 = (f32[288,896]{1,0:T(8,128)S(1)}, f32[288,896]{1,0:T(8,128)}, u32[]{:S(2)}, u32[]{:S(2)}) collective-permute-start(f32[288,896]{1,0:T(8,128)S(1)} %collective-permute-done.20.refs_7_), channel_id=1, source_target_pairs={{8,0},{16,24},{9,1},{17,25},{10,2},{18,26},{11,3},{19,27},{12,4},{... | collective-permute-start | bytes 3096584 | tf_op jit(solution)/shard_map/ppermute | solution.py:604
  40.8 76.6 %collective-permute-start.15 = (f32[288,896]{1,0:T(8,128)}, f32[288,896]{1,0:T(8,128)}, u32[]{:S(2)}, u32[]{:S(2)}) collective-permute-start(f32[288,896]{1,0:T(8,128)} %get-tuple-element.119), channel_id=1, source_target_pairs={{0,8},{24,16},{1,9},{25,17},{2,10},{26,18},{3,11},{27,19},{4,12},{... | collective-permute-start | bytes 3096584 | tf_op jit(solution)/shard_map/ppermute | solution.py:601
  46.0 71.3 %collective-permute-start.16 = (f32[288,896]{1,0:T(8,128)}, f32[288,896]{1,0:T(8,128)}, u32[]{:S(2)}, u32[]{:S(2)}) collective-permute-start(f32[288,896]{1,0:T(8,128)} %get-tuple-element.120), channel_id=1, source_target_pairs={{0,16},{24,8},{1,17},{25,9},{2,18},{26,10},{3,19},{27,11},{4,20},{... | collective-permute-start | bytes 3096584 | tf_op jit(solution)/shard_map/ppermute | solution.py:601
  48.3 69.1 %collective-permute-start.17 = (f32[288,896]{1,0:T(8,128)}, f32[288,896]{1,0:T(8,128)}, u32[]{:S(2)}, u32[]{:S(2)}) collective-permute-start(f32[288,896]{1,0:T(8,128)} %get-tuple-element.121), channel_id=1, source_target_pairs={{8,16},{16,8},{9,17},{17,9},{10,18},{18,10},{11,19},{19,11},{12,20... | collective-permute-start | bytes 3096584 | tf_op jit(solution)/shard_map/ppermute | solution.py:601
  57.8 23.9 %collective-permute-start.19 = (f32[288,896]{1,0:T(8,128)S(1)}, f32[288,896]{1,0:T(8,128)}, u32[]{:S(2)}, u32[]{:S(2)}) collective-permute-start(f32[288,896]{1,0:T(8,128)S(1)} %collective-permute-done.18.refs_6_), channel_id=1, source_target_pairs={{8,0},{16,24},{9,1},{17,25},{10,2},{18,26},{11,3},{19,27},{12,4},{... | collective-permute-start | bytes 3096584 | tf_op jit(solution)/shard_map/ppermute | solution.py:604
  59.2 75.5 %collective-permute-start.25 = (f32[288,896]{1,0:T(8,128)}, f32[288,896]{1,0:T(8,128)S(1)}, u32[]{:S(2)}, u32[]{:S(2)}) collective-permute-start(f32[288,896]{1,0:T(8,128)} %get-tuple-element.131), channel_id=1, source_target_pairs={{8,24},{16,0},{9,25},{17,1},{10,26},{18,2},{11,27},{19,3},{12,28},... | collective-permute-start | bytes 3096584 | tf_op jit(solution)/shard_map/ppermute | solution.py:604
  81.7 35.7 %copy-start.4 = (f32[288,896]{1,0:T(8,128)S(1)}, f32[288,896]{1,0:T(8,128)}, u32[]{:S(2)}) copy-start(f32[288,896]{1,0:T(8,128)} %get-tuple-element.118) | copy-start | bytes 3096580
  87.6 27.9 %copy-start.2 = (bf16[4,576,896]{2,1,0:T(8,128)(2,1)}, bf16[4,576,896]{2,1,0:T(8,128)(2,1)S(1)}, u32[]{:S(2)}) copy-start(bf16[4,576,896]{2,1,0:T(8,128)(2,1)S(1)} %get-tuple-element.144.refs_6_) | copy-start | bytes 12386308 | tf_op jit(solution)/shard_map/cond
  87.6 1.9 collective-permute-start
  89.5 8.4 %collective-permute-start.1 = (f32[288,384]{1,0:T(8,128)S(1)}, f32[288,384]{1,0:T(8,128)S(1)}, u32[]{:S(2)}, u32[]{:S(2)}) collective-permute-start(f32[288,384]{1,0:T(8,128)S(1)} %add.22), channel_id=1, source_target_pairs={{0,2},{1,5},{2,0},{3,7},{4,6},{5,1},{6,4},{7,3},{8,10},{9,13},{10,... | collective-permute-start | bytes 1327112 | tf_op jit(solution)/shard_map/cond/branch_0_fun/ppermute | solution.py:578
  98.0 8.4 %collective-permute-start.2 = (f32[288,384]{1,0:T(8,128)S(1)}, f32[288,384]{1,0:T(8,128)S(1)}, u32[]{:S(2)}, u32[]{:S(2)}) collective-permute-start(f32[288,384]{1,0:T(8,128)S(1)} %add.23), channel_id=1, source_target_pairs={{0,4},{1,3},{2,6},{3,1},{4,0},{5,7},{6,2},{7,5},{8,12},{9,11},{10,... | collective-permute-start | bytes 1327112 | tf_op jit(solution)/shard_map/cond/branch_0_fun/ppermute | solution.py:578
  106.4 1.9 collective-permute-start.3
  115.7 19.1 %collective-permute-start.26 = (f32[288,896]{1,0:T(8,128)}, f32[288,896]{1,0:T(8,128)}, u32[]{:S(2)}, u32[]{:S(2)}) collective-permute-start(f32[288,896]{1,0:T(8,128)} %get-tuple-element.132), channel_id=1, source_target_pairs={{8,16},{16,8},{9,17},{17,9},{10,18},{18,10},{11,19},{19,11},{12,20... | collective-permute-start | bytes 3096584 | tf_op jit(solution)/shard_map/ppermute | solution.py:604
  117.4 51.3 %collective-permute-start.24 = (f32[288,896]{1,0:T(8,128)}, f32[288,896]{1,0:T(8,128)S(1)}, u32[]{:S(2)}, u32[]{:S(2)}) collective-permute-start(f32[288,896]{1,0:T(8,128)} %get-tuple-element.127), channel_id=1, source_target_pairs={{8,24},{16,0},{9,25},{17,1},{10,26},{18,2},{11,27},{19,3},{12,28},... | collective-permute-start | bytes 3096584 | tf_op jit(solution)/shard_map/ppermute | solution.py:604
  118.7 51.5 %collective-permute-start.23 = (f32[288,896]{1,0:T(8,128)}, f32[288,896]{1,0:T(8,128)S(1)}, u32[]{:S(2)}, u32[]{:S(2)}) collective-permute-start(f32[288,896]{1,0:T(8,128)} %get-tuple-element.126), channel_id=1, source_target_pairs={{8,16},{16,8},{9,17},{17,9},{10,18},{18,10},{11,19},{19,11},{12,20... | collective-permute-start | bytes 3096584 | tf_op jit(solution)/shard_map/ppermute | solution.py:604
  119.5 71.3 %collective-permute-start.22 = (f32[288,896]{1,0:T(8,128)}, f32[288,896]{1,0:T(8,128)S(1)}, u32[]{:S(2)}, u32[]{:S(2)}) collective-permute-start(f32[288,896]{1,0:T(8,128)} %get-tuple-element.125), channel_id=1, source_target_pairs={{8,0},{16,24},{9,1},{17,25},{10,2},{18,26},{11,3},{19,27},{12,4},{... | collective-permute-start | bytes 3096584 | tf_op jit(solution)/shard_map/ppermute | solution.py:604
  127.4 7.4 %copy-start.8 = (s32[4]{0:T(128)S(1)}, s32[4]{0:T(128)}, u32[]{:S(2)}) copy-start(s32[4]{0:T(128)} %refs_0_.15) | copy-start | bytes 52
  (2 other events, 1.3 us)
